TPU v7x, 128 devices: a whole 4x4x4 slice. The times are simulated.
128 devices in a mesh: dp: 8 (over z, x_lo), tensor: 8 (over x_hi, y), pre: 2 (over core).
Axes of the slice: x: 4 (x_hi: 2, x_lo: 2; x = x_hi * 2 + x_lo), y: 4, z: 4, core: 2. Of those that a mesh axis runs over, the one named last changes fastest.
Arguments:
- tokens: bfloat16 [8192, 4096], P('dp', ('tensor', 'pre')), may hold values from -6 to 6
- weight: bfloat16 [4096, 16384], P('dp', ('tensor', 'pre')), may hold values from -0.09375 to 0.09375
- cotangent: bfloat16 [8192, 16384], P('dp', ('tensor', 'pre')), may hold values from -6 to 6
- left_stats: float32 [8, 32, 512, 512], P('dp', ('tensor', 'pre')), as said below
- right_stats: float32 [8, 32, 512, 512], P('dp', ('tensor', 'pre')), as said below
Outputs:
- tokens_grad: bfloat16 [8192, 4096], P('dp', ('tensor', 'pre'))
- update: bfloat16 [4096, 16384], P('dp', ('tensor', 'pre'))
- left_new: float32 [8, 32, 512, 512], P('dp', ('tensor', 'pre'))
- right_new: float32 [8, 32, 512, 512], P('dp', ('tensor', 'pre'))
Inputs may be any that keep to these rules, and one draw needn't show every extreme that they name: `left_stats`: each block is symmetric positive definite. `right_stats`: each block is symmetric positive definite.
All inputs are finite; a program needn't handle non-finite values.
Results may differ from a plain program's by a relative error of at most 0.02.
Values may be sent and summed in bfloat16 or wider, within the bound.
A program may use at most 192 MiB of HBM per device.

v0:
```python
import jax
import jax.numpy as jnp
from jax import lax
from jax.sharding import PartitionSpec as P

ITERS = 3


decay_rate = 0.5
ridge_share = 0.05
epsilon = 1e-06


def gelu_slope(values):
    return (
        0.5 * (1.0 + lax.erf(values * 0.7071067811865476))
        + values * jnp.exp(-0.5 * values * values) * 0.3989422804014327
    )


def matmul_high(left, right):
    return jnp.einsum("kij,kjl->kil", left, right, precision=lax.Precision.HIGHEST)


def newton_roots(statistic):
    size = statistic.shape[-1]
    identity_mat = jnp.eye(size, dtype=jnp.float32)
    trace_val = jnp.sum(statistic * identity_mat, axis=(1, 2), keepdims=True)
    regular = statistic + ridge_share * (trace_val / size) * identity_mat
    norm_scale = jnp.sqrt(jnp.sum(regular * regular, axis=(1, 2), keepdims=True)) / 4.0
    current = regular / norm_scale
    inverse_root = identity_mat
    for sweep in range(ITERS):
        step_mat = (5.0 * identity_mat - current) / 4.0
        if sweep == 0:
            inverse_root = norm_scale ** (-0.25) * step_mat
        else:
            inverse_root = matmul_high(inverse_root, step_mat)
        if sweep + 1 < ITERS:
            square = matmul_high(step_mat, step_mat)
            current = matmul_high(matmul_high(square, square), current)
    return inverse_root.astype(jnp.bfloat16)


def shards(tokens, weight, cotangent, left_stats, right_stats):
    features_all = lax.all_gather(tokens, ("tensor", "pre"), axis=1, tiled=True)
    tok_rows = tokens.shape[0]
    hidden = jnp.dot(
        features_all,
        lax.all_gather(weight, "dp", axis=0, tiled=True),
        preferred_element_type=jnp.float32,
    )
    hidden_grad = (cotangent.astype(jnp.float32) * gelu_slope(hidden)).astype(jnp.bfloat16)
    input_part = lax.dot_general(
        hidden_grad,
        lax.all_gather(weight, "dp", axis=0, tiled=True),
        (((1,), (1,)), ((), ())),
        preferred_element_type=jnp.float32,
    )
    tokens_grad = lax.psum_scatter(
        input_part.astype(jnp.bfloat16), ("tensor", "pre"), scatter_dimension=1, tiled=True
    )
    dp_count = lax.axis_size("dp")
    grad_scale = float(tok_rows * dp_count) ** (-0.5)
    grad_part = (
        lax.dot_general(
            features_all, hidden_grad, (((0,), (0,)), ((), ())), preferred_element_type=jnp.float32
        )
        * grad_scale
    )
    grad = lax.psum_scatter(
        grad_part.astype(jnp.bfloat16), "dp", scatter_dimension=0, tiled=True
    ).astype(jnp.float32)
    row_count = left_stats.shape[0]
    col_count = left_stats.shape[1]
    size = left_stats.shape[2]
    count = row_count * col_count
    blocks = (
        grad.reshape(row_count, size, col_count, size)
        .transpose(0, 2, 1, 3)
        .reshape(count, size, size)
    )
    left_old = left_stats.reshape(count, size, size)
    right_old = right_stats.reshape(count, size, size)
    left_new = decay_rate * left_old + (1.0 - decay_rate) / size * jnp.einsum(
        "kij,klj->kil", blocks, blocks, precision=lax.Precision.HIGHEST
    )
    right_new = decay_rate * right_old + (1.0 - decay_rate) / size * jnp.einsum(
        "kji,kjl->kil", blocks, blocks, precision=lax.Precision.HIGHEST
    )
    statistic = jnp.concatenate([left_new, right_new], axis=0)
    roots_all = newton_roots(statistic)
    left_root = roots_all[:count]
    right_root = roots_all[count:]
    grad_half = blocks.astype(jnp.bfloat16)
    left_part = jnp.einsum(
        "kij,kjl->kil", left_root, grad_half, preferred_element_type=jnp.float32
    ).astype(jnp.bfloat16)
    raw = jnp.einsum("kij,kjl->kil", left_part, right_root, preferred_element_type=jnp.float32)
    grad_rms = jnp.sqrt(jnp.mean(blocks * blocks, axis=(1, 2), keepdims=True))
    raw_rms = jnp.sqrt(jnp.mean(raw * raw, axis=(1, 2), keepdims=True) + epsilon)
    update_blocks = (raw * grad_rms / raw_rms).astype(jnp.bfloat16)
    update = (
        update_blocks.reshape(row_count, col_count, size, size)
        .transpose(0, 2, 1, 3)
        .reshape(row_count * size, col_count * size)
    )
    left_out = left_new.reshape(row_count, col_count, size, size)
    right_out = right_new.reshape(row_count, col_count, size, size)
    return (tokens_grad, update, left_out, right_out)


def solution(mesh):
    return jax.shard_map(
        shards,
        mesh=mesh,
        in_specs=(
            P("dp", ("tensor", "pre")),
            P("dp", ("tensor", "pre")),
            P("dp", ("tensor", "pre")),
            P("dp", ("tensor", "pre"), None, None),
            P("dp", ("tensor", "pre"), None, None),
        ),
        out_specs=(
            P("dp", ("tensor", "pre")),
            P("dp", ("tensor", "pre")),
            P("dp", ("tensor", "pre"), None, None),
            P("dp", ("tensor", "pre"), None, None),
        ),
        check_vma=False,
    )
```

profile of v0, /device:TPU:0, one launch (start us, length us, event | category | flops | bytes accessed | tf_op | source)
XLA Modules:
  0.0 570.1 jit_solution(502088741170493349)
XLA Ops:
  7.2 0.7 all-gather.5.cloned.1.call-update
  7.9 0.7 all-gather.3.cloned.1.call-update
  8.7 171.8 %all-gather.5.cloned.1.call-done = bf16[4096,1024]{1,0:T(8,128)(2,1)} async-done(((bf16[512,1024]{1,0:T(8,128)(2,1)}), bf16[4096,1024]{1,0:T(8,128)(2,1)}) %all-gather.5.cloned.1.call-update) | async-done | bytes 8388624 | tf_op jit(solution)/shard_map/all_gather | solution.py:50
  180.5 80.3 %all-gather.3.cloned.1.call-done = bf16[1024,4096]{1,0:T(8,128)(2,1)} async-done(((bf16[1024,256]{1,0:T(8,128)(2,1)}), bf16[1024,4096]{1,0:T(8,128)(2,1)}) %all-gather.3.cloned.1.call-update) | async-done | bytes 8388624 | tf_op jit(solution)/shard_map/all_gather | solution.py:46
  260.8 12.8 %fusion.44 = f32[1024,1024]{1,0:T(8,128)S(1)} fusion(bf16[1024,4096]{1,0:T(8,128)(2,1)} %all-gather.3.cloned.1.call-done, bf16[4096,1024]{1,0:T(8,128)(2,1)} %all-gather.5.cloned.1.call-done), kind=kOutput, calls=%fused_computation.57 | convolution fusion | flops 8589934592 | bytes 20971520 | tf_op jit(solution)/shard_map/dot_general | solution.py:48
  273.6 1.9 copy-done.9
  275.5 12.9 %fusion = bf16[4096,1024]{0,1:T(8,128)(2,1)} fusion(bf16[1024,4096]{1,0:T(8,128)(2,1)S(1)} %copy-done.7, f32[1024,1024]{1,0:T(8,128)S(1)} %fusion.44, bf16[1024,1024]{1,0:T(8,128)(2,1)S(1)} %copy-done.8), kind=kOutput, calls=%fused_computation.2 | convolution fusion | flops 8609857536 | bytes 23068672 | tf_op jit(solution)/shard_map/dot_general | solution.py:66
  288.4 0.5 reduce-scatter.3.cloned.1.call-start
  288.9 15.9 %convolution_convert_fusion = bf16[1024,4096]{1,0:T(8,128)(2,1)} fusion(bf16[4096,1024]{1,0:T(8,128)(2,1)} %all-gather.5.cloned.1.call-done, f32[1024,1024]{1,0:T(8,128)} %copy-done.9, bf16[1024,1024]{1,0:T(8,128)(2,1)S(1)} %copy-done.8), kind=kOutput, calls=%fused_computation.1 | convolution fusion | flops 8605663232 | bytes 23068672 | tf_op jit(solution)/shard_map/dot_general | solution.py:54
  304.8 1.1 fusion.33
  305.9 1.1 fusion.32
  307.0 148.3 %reduce-scatter.5.cloned.1.call-done = bf16[512,1024]{0,1:T(8,128)(2,1)} async-done(((bf16[4096,1024]{0,1:T(8,128)(2,1)}), bf16[512,1024]{0,1:T(8,128)(2,1)}) %reduce-scatter.5.cloned.1.call-update) | async-done | bytes 1048592 | tf_op jit(solution)/shard_map/reduce_scatter | solution.py:71
  455.3 1.6 multiply_reduce_fusion.3
  456.9 0.1 reduce_sum.47
  457.1 2.5 bitcast_add_fusion
  459.6 0.8 bitcast_add_fusion.1
  460.4 1.1 copy-done.4
  461.5 0.7 multiply_reduce_fusion.1
  462.2 1.4 multiply_reduce_fusion
  463.7 8.7 %fusion.10 = f32[4,512,512]{2,1,0:T(8,128)S(1)} fusion(f32[512,512]{1,0:T(8,128)S(1)} %copy-done.3, f32[2,512,512]{2,1,0:T(8,128)S(1)} %bitcast_add_fusion, f32[2,512,512]{2,1,0:T(8,128)S(1)} %bitcast_add_fusion.1, f32[4]{0:T(128)S(1)} %get-tuple-element.13, f32[4]{0:T(128)S(1)} %broadcast_multiply_fusion, f32[512,512]{1,0:T(8,128)S(1)} %copy-done.4), kind=kOutput, calls=%fused_computation.15 | convolution fusion | flops 6448742400 | bytes 10485792 | tf_op jit(solution)/shard_map/kij,kjl->kil/dot_general | solution.py:22
  472.3 7.6 %fusion.45 = f32[4,512,512]{2,1,0:T(8,128)S(1)} fusion(f32[4,512,512]{2,1,0:T(8,128)S(1)} %fusion.10), kind=kOutput, calls=%fused_computation.58 | convolution fusion | flops 6442450944 | bytes 8388608 | tf_op jit(solution)/shard_map/kij,kjl->kil/dot_general | solution.py:22
  479.9 8.1 %fusion.41 = f32[4,512,512]{2,1,0:T(8,128)S(1)} fusion(f32[4,512,512]{2,1,0:T(8,128)S(1)} %fusion.45, f32[2,512,512]{2,1,0:T(8,128)S(1)} %bitcast_add_fusion, f32[2,512,512]{2,1,0:T(8,128)S(1)} %bitcast_add_fusion.1, f32[4]{0:T(128)S(1)} %get-tuple-element.13, f32[4]{0:T(128)S(1)} %broadcast_multiply_fusion, f32[512,512]{1,0:T(8,128)S(1)} %copy-done.4), kind=kOutput, calls=%fused_computation.56 | convolution fusion | flops 6446645248 | bytes 13631520 | tf_op jit(solution)/shard_map/kij,kjl->kil/dot_general | solution.py:22
  488.0 7.7 %fusion.17 = f32[4,512,512]{2,1,0:T(8,128)S(1)} fusion(f32[4,512,512]{2,1,0:T(8,128)S(1)} %fusion.41, f32[512,512]{1,0:T(8,128)S(1)} %copy-done.3), kind=kOutput, calls=%fused_computation.25 | convolution fusion | flops 6444548096 | bytes 9437184 | tf_op jit(solution)/shard_map/kij,kjl->kil/dot_general | solution.py:22
  495.8 7.5 %fusion.46 = f32[4,512,512]{2,1,0:T(8,128)S(1)} fusion(f32[4,512,512]{2,1,0:T(8,128)S(1)} %fusion.17), kind=kOutput, calls=%fused_computation.59 | convolution fusion | flops 6442450944 | bytes 8388608 | tf_op jit(solution)/shard_map/kij,kjl->kil/dot_general | solution.py:22
  503.3 7.4 %fusion.47 = f32[4,512,512]{2,1,0:T(8,128)S(1)} fusion(f32[4,512,512]{2,1,0:T(8,128)S(1)} %fusion.46, f32[4,512,512]{2,1,0:T(8,128)S(1)} %fusion.41), kind=kOutput, calls=%fused_computation.60 | convolution fusion | flops 6442450944 | bytes 12582912 | tf_op jit(solution)/shard_map/kij,kjl->kil/dot_general | solution.py:22
  510.7 8.4 %fusion.12 = f32[4,512,512]{2,1,0:T(8,128)S(1)} fusion(f32[4,512,512]{2,1,0:T(8,128)S(1)} %fusion.41, f32[4]{0:T(128)S(1)} %get-tuple-element.12, f32[512,512]{1,0:T(8,128)S(1)} %copy-done.3, f32[2,512,512]{2,1,0:T(8,128)S(1)} %bitcast_add_fusion, f32[2,512,512]{2,1,0:T(8,128)S(1)} %bitcast_add_fusion.1, f32[4]{0:T(128)S(1)} %get-tuple-element.13, ...), kind=kOutput, calls=%fused_computation.17 | convolution fusion | flops 6450839552 | bytes 14680112 | tf_op jit(solution)/shard_map/kij,kjl->kil/dot_general | solution.py:22
  519.1 7.4 %fusion.27 = bf16[4,512,512]{2,1,0:T(8,128)(2,1)S(1)} fusion(f32[4,512,512]{2,1,0:T(8,128)S(1)} %fusion.12, f32[4,512,512]{2,1,0:T(8,128)S(1)} %fusion.47, f32[512,512]{1,0:T(8,128)S(1)} %copy-done.3), kind=kOutput, calls=%fused_computation.40 | convolution fusion | flops 6445596672 | bytes 11534336 | tf_op jit(solution)/shard_map/kij,kjl->kil/dot_general | solution.py:22
  526.5 0.7 convolution_convert_fusion.1
  527.2 1.0 multiply_reduce_fusion.2
  528.2 0.4 divide_convert_fusion
  528.6 1.3 copy.18
  529.9 33.5 %reduce-scatter.3.cloned.1.call-done = bf16[1024,256]{1,0:T(8,128)(2,1)} async-done(((bf16[1024,4096]{1,0:T(8,128)(2,1)}), bf16[1024,256]{1,0:T(8,128)(2,1)}) %reduce-scatter.3.cloned.1.call-update) | async-done | bytes 524304 | tf_op jit(solution)/shard_map/reduce_scatter | solution.py:60
  (27 shorter events, 0.2 us)
Async XLA Ops:
  7.2 173.3 %all-gather.5.cloned.1.call-start = ((), (), s32[]{:S(2)}) async-start(), calls=%async_computation.3 | async-start | bytes 9437184 | tf_op jit(solution)/shard_map/all_gather | solution.py:50
  7.9 252.9 %all-gather.3.cloned.1.call-start = ((), (), s32[]{:S(2)}) async-start(), calls=%async_computation.2 | async-start | bytes 8912896 | tf_op jit(solution)/shard_map/all_gather | solution.py:46
  8.6 266.9 %copy-start.8 = (bf16[1024,1024]{1,0:T(8,128)(2,1)S(1)}, bf16[1024,1024]{1,0:T(8,128)(2,1)}, u32[]{:S(2)}) copy-start(bf16[1024,1024]{1,0:T(8,128)(2,1)} %param.7) | copy-start | bytes 6291460
  8.7 446.7 %reduce-scatter.5.cloned.1.call-start = ((), (), s32[]{:S(2)}) async-start(), calls=%async_computation.5 | async-start | bytes 9437184 | tf_op jit(solution)/shard_map/reduce_scatter | solution.py:71
  260.8 14.7 %copy-start.7 = (bf16[1024,4096]{1,0:T(8,128)(2,1)S(1)}, bf16[1024,4096]{1,0:T(8,128)(2,1)}, u32[]{:S(2)}) copy-start(bf16[1024,4096]{1,0:T(8,128)(2,1)} %all-gather.3.cloned.1.call-done) | copy-start | bytes 25165828
  273.6 1.9 copy-start.9
  288.4 274.9 %reduce-scatter.3.cloned.1.call-start = ((), (), s32[]{:S(2)}) async-start(), calls=%async_computation.4 | async-start | bytes 8912896 | tf_op jit(solution)/shard_map/reduce_scatter | solution.py:60
  304.8 152.3 %copy-start.5 = (f32[1,2,512,512]{3,2,1,0:T(8,128)S(1)}, f32[1,2,512,512]{3,2,1,0:T(8,128)}, u32[]{:S(2)}) copy-start(f32[1,2,512,512]{3,2,1,0:T(8,128)} %param.9) | copy-start | bytes 6291460
  455.3 4.2 copy-start
  457.0 2.5 copy-start.6
  459.5 51.1 %copy-start.1 = (f32[2,512,512]{2,1,0:T(8,128)}, f32[2,512,512]{2,1,0:T(8,128)S(1)}, u32[]{:S(2)}) copy-start(f32[2,512,512]{2,1,0:T(8,128)S(1)} %bitcast_add_fusion) | copy-start | bytes 6291460
  459.6 2.0 copy-start.4
  461.5 49.1 %copy-start.2 = (f32[2,512,512]{2,1,0:T(8,128)}, f32[2,512,512]{2,1,0:T(8,128)S(1)}, u32[]{:S(2)}) copy-start(f32[2,512,512]{2,1,0:T(8,128)S(1)} %bitcast_add_fusion.1) | copy-start | bytes 6291460
  461.5 2.1 copy-start.3
Sparse Core Ops, SparseCore 0:
  9.6 170.7 all-gather.4
  182.8 78.0 all-gather.2
  288.5 166.7 reduce-scatter.4
  460.0 103.3 reduce-scatter.2
where the time goes:
time: 576 us; the launch traced here: 570 us
  waiting for transfers between devices  435 us (76%)
  matrix products  109 us (19%)
  between operations  14.2 us (2%)
  other arithmetic  6.35 us (1%)
    all_gather x1, waiting for transfers between devices, shards(): lax.all_gather(weight, 'dp', axis=0, tiled=True)  172 us
    reduce_scatter x1, waiting for transfers between devices, shards(): lax.psum_scatter(grad_part.astype(jnp.bfloat16), 'dp', scatter_dimension=...  148 us
    all_gather x1, waiting for transfers between devices, shards(): features_all = lax.all_gather(tokens, ('tensor', 'pre'), axis=1, tiled=True)  80.3 us
    dot_general x8, matrix products, matmul_high(): jnp.einsum('kij,kjl->kil', left, right, precision=lax.Precision.HIGHEST)  62.7 us
    reduce_scatter x1, waiting for transfers between devices, shards(): lax.psum_scatter(input_part.astype(jnp.bfloat16), ('tensor', 'pre'), scat...  33.5 us
    dot_general x1, matrix products, shards(): lax.dot_general(hidden_grad, lax.all_gather(weight, 'dp', axis=0, tiled=T...  15.9 us
    dot_general x1, matrix products, shards(): lax.dot_general(features_all, hidden_grad, (((0,), (0,)), ((), ())), pref...  12.9 us
    dot_general x1, matrix products, shards(): jnp.dot(features_all, lax.all_gather(weight, 'dp', axis=0, tiled=True), p...  12.8 us
  transfers between devices with their start and end apart: 4, of which 4 were waited for; matrix products, arithmetic and copies ran while one was open for 16% of the time, Pallas kernels for 0%

commit v1 on v0

--- a/solution.py
+++ b/solution.py
@@ -18,8 +18,13 @@
     )
 
 
-def matmul_high(left, right):
-    return jnp.einsum("kij,kjl->kil", left, right, precision=lax.Precision.HIGHEST)
+def product(left, right):
+    return jnp.einsum(
+        "kij,kjl->kil",
+        left.astype(jnp.bfloat16),
+        right.astype(jnp.bfloat16),
+        preferred_element_type=jnp.float32,
+    )
 
 
 def newton_roots(statistic):
@@ -28,32 +33,33 @@
     trace_val = jnp.sum(statistic * identity_mat, axis=(1, 2), keepdims=True)
     regular = statistic + ridge_share * (trace_val / size) * identity_mat
     norm_scale = jnp.sqrt(jnp.sum(regular * regular, axis=(1, 2), keepdims=True)) / 4.0
-    current = regular / norm_scale
-    inverse_root = identity_mat
-    for sweep in range(ITERS):
-        step_mat = (5.0 * identity_mat - current) / 4.0
-        if sweep == 0:
-            inverse_root = norm_scale ** (-0.25) * step_mat
-        else:
-            inverse_root = matmul_high(inverse_root, step_mat)
-        if sweep + 1 < ITERS:
-            square = matmul_high(step_mat, step_mat)
-            current = matmul_high(matmul_high(square, square), current)
-    return inverse_root.astype(jnp.bfloat16)
+    first = regular / norm_scale
+    square = product(first, first)
+    step_zero = 1.25 * identity_mat - 0.25 * first
+    step_zero_sq = 1.5625 * identity_mat - 0.625 * first + 0.0625 * square
+    fourth = product(step_zero_sq, step_zero_sq)
+    crossed = 1.25 * first - 0.25 * square
+    root_two = 1.25 * step_zero - 0.25 * product(fourth, crossed)
+    two_sq = product(root_two, root_two)
+    two_fourth = product(two_sq, two_sq)
+    two_crossed = product(root_two, first)
+    root_three = 1.25 * root_two - 0.25 * product(two_fourth, two_crossed)
+    return (norm_scale ** (-0.25) * root_three).astype(jnp.bfloat16)
 
 
 def shards(tokens, weight, cotangent, left_stats, right_stats):
     features_all = lax.all_gather(tokens, ("tensor", "pre"), axis=1, tiled=True)
     tok_rows = tokens.shape[0]
+    weight_all = lax.all_gather(weight, "dp", axis=0, tiled=True)
     hidden = jnp.dot(
         features_all,
-        lax.all_gather(weight, "dp", axis=0, tiled=True),
+        weight_all,
         preferred_element_type=jnp.float32,
     )
     hidden_grad = (cotangent.astype(jnp.float32) * gelu_slope(hidden)).astype(jnp.bfloat16)
     input_part = lax.dot_general(
         hidden_grad,
-        lax.all_gather(weight, "dp", axis=0, tiled=True),
+        weight_all,
         (((1,), (1,)), ((), ())),
         preferred_element_type=jnp.float32,
     )
@@ -82,11 +88,11 @@
     )
     left_old = left_stats.reshape(count, size, size)
     right_old = right_stats.reshape(count, size, size)
-    left_new = decay_rate * left_old + (1.0 - decay_rate) / size * jnp.einsum(
-        "kij,klj->kil", blocks, blocks, precision=lax.Precision.HIGHEST
+    left_new = decay_rate * left_old + (1.0 - decay_rate) / size * product(
+        blocks, blocks.transpose(0, 2, 1)
     )
-    right_new = decay_rate * right_old + (1.0 - decay_rate) / size * jnp.einsum(
-        "kji,kjl->kil", blocks, blocks, precision=lax.Precision.HIGHEST
+    right_new = decay_rate * right_old + (1.0 - decay_rate) / size * product(
+        blocks.transpose(0, 2, 1), blocks
     )
     statistic = jnp.concatenate([left_new, right_new], axis=0)
     roots_all = newton_roots(statistic)

time: 576 us -> 570 us (0.990); the launches traced: 570 us -> 570 us
  waiting for transfers between devices: 435 us -> 455 us
  matrix products: 109 us -> 90.2 us
    dot_general x12 -> x8, matrix products: 94.6 us -> 74.2 us  [the longest x6 45.5 us: product(): jnp.einsum('kij,kjl->kil', left.astype(jnp.bfloat16), right.astype(jnp.bf...]
    reduce_scatter x1, waiting for transfers between devices: 33.5 us -> 53.6 us  [shards(): lax.psum_scatter(input_part.astype(jnp.bfloat16), ('tensor', 'pre'), scat...]
  transfers between devices with their start and end apart: 4 -> 4, of which waited for: 4 -> 4; matrix products, arithmetic and copies ran while one was open for 16% -> 13% of each run, Pallas kernels for 0% -> 0%
where the time goes in v1:
time: 570 us
  waiting for transfers between devices  455 us (80%)
  matrix products  90.2 us (16%)
  between operations  13.9 us (2%)
  other arithmetic  7.01 us (1%)
    all_gather x1, waiting for transfers between devices, shards(): weight_all = lax.all_gather(weight, 'dp', axis=0, tiled=True)  172 us
    reduce_scatter x1, waiting for transfers between devices, shards(): lax.psum_scatter(grad_part.astype(jnp.bfloat16), 'dp', scatter_dimension=...  148 us
    all_gather x1, waiting for transfers between devices, shards(): features_all = lax.all_gather(tokens, ('tensor', 'pre'), axis=1, tiled=True)  80.3 us
    reduce_scatter x1, waiting for transfers between devices, shards(): lax.psum_scatter(input_part.astype(jnp.bfloat16), ('tensor', 'pre'), scat...  53.6 us
    dot_general x6, matrix products, product(): jnp.einsum('kij,kjl->kil', left.astype(jnp.bfloat16), right.astype(jnp.bf...  45.5 us
    dot_general x1, matrix products, shards(): lax.dot_general(hidden_grad, weight_all, (((1,), (1,)), ((), ())), prefer...  15.9 us
    dot_general x1, matrix products, shards(): lax.dot_general(features_all, hidden_grad, (((0,), (0,)), ((), ())), pref...  12.9 us
    dot_general x1, matrix products, shards(): jnp.dot(features_all, weight_all, preferred_element_type=jnp.float32)  12.8 us
  transfers between devices with their start and end apart: 4, of which 4 were waited for; matrix products, arithmetic and copies ran while one was open for 13% of the time, Pallas kernels for 0%

profile of v1, /device:TPU:0, one launch (start us, length us, event | category | flops | bytes accessed | tf_op | source)
XLA Modules:
  0.0 569.9 jit_solution(3450052099851821384)
XLA Ops:
  7.2 0.0 all-gather.5.cloned.1.call-start
  7.2 0.7 all-gather.5.cloned.1.call-update
  7.9 0.0 all-gather.3.cloned.1.call-start
  7.9 0.7 all-gather.3.cloned.1.call-update
  8.7 0.0 reduce-scatter.5.cloned.1.call-start
  8.7 171.8 %all-gather.5.cloned.1.call-done = bf16[4096,1024]{1,0:T(8,128)(2,1)} async-done(((bf16[512,1024]{1,0:T(8,128)(2,1)}), bf16[4096,1024]{1,0:T(8,128)(2,1)}) %all-gather.5.cloned.1.call-update) | async-done | bytes 8388624 | tf_op jit(solution)/shard_map/all_gather | solution.py:53
  180.5 80.3 %all-gather.3.cloned.1.call-done = bf16[1024,4096]{1,0:T(8,128)(2,1)} async-done(((bf16[1024,256]{1,0:T(8,128)(2,1)}), bf16[1024,4096]{1,0:T(8,128)(2,1)}) %all-gather.3.cloned.1.call-update) | async-done | bytes 8388624 | tf_op jit(solution)/shard_map/all_gather | solution.py:51
  260.8 12.8 %fusion.52 = f32[1024,1024]{1,0:T(8,128)S(1)} fusion(bf16[1024,4096]{1,0:T(8,128)(2,1)} %all-gather.3.cloned.1.call-done, bf16[4096,1024]{1,0:T(8,128)(2,1)} %all-gather.5.cloned.1.call-done), kind=kOutput, calls=%fused_computation.58 | convolution fusion | flops 8589934592 | bytes 20971520 | tf_op jit(solution)/shard_map/dot_general | solution.py:54
  273.6 1.9 copy-done.7
  275.5 12.9 %fusion = bf16[4096,1024]{0,1:T(8,128)(2,1)} fusion(bf16[1024,4096]{1,0:T(8,128)(2,1)S(1)} %copy-done.4, f32[1024,1024]{1,0:T(8,128)S(1)} %fusion.52, bf16[1024,1024]{1,0:T(8,128)(2,1)S(1)} %copy-done.5), kind=kOutput, calls=%fused_computation.2 | convolution fusion | flops 8609857536 | bytes 23068672 | tf_op jit(solution)/shard_map/dot_general | solution.py:72
  288.4 0.0 reduce-scatter.5.cloned.1.call-update
  288.4 0.2 reduce-scatter.3.cloned.1.call-start
  288.7 15.9 %convolution_convert_fusion = bf16[1024,4096]{1,0:T(8,128)(2,1)} fusion(bf16[4096,1024]{1,0:T(8,128)(2,1)} %all-gather.5.cloned.1.call-done, f32[1024,1024]{1,0:T(8,128)} %copy-done.7, bf16[1024,1024]{1,0:T(8,128)(2,1)S(1)} %copy-done.5), kind=kOutput, calls=%fused_computation.1 | convolution fusion | flops 8605663232 | bytes 23068672 | tf_op jit(solution)/shard_map/dot_general | solution.py:60
  304.6 0.0 reduce-scatter.3.cloned.1.call-update
  304.6 1.1 fusion.38
  305.7 1.6 fusion.36
  307.3 148.0 %reduce-scatter.5.cloned.1.call-done = bf16[512,1024]{0,1:T(8,128)(2,1)} async-done(((bf16[4096,1024]{0,1:T(8,128)(2,1)}), bf16[512,1024]{0,1:T(8,128)(2,1)}) %reduce-scatter.5.cloned.1.call-update) | async-done | bytes 1048592 | tf_op jit(solution)/shard_map/reduce_scatter | solution.py:77
  455.3 1.6 multiply_reduce_fusion.3
  456.9 0.1 reduce_sum.47
  457.1 3.0 bitcast_add_fusion
  460.1 3.2 bitcast_add_fusion.1
  463.3 0.8 multiply_reduce_fusion.1
  464.2 1.4 multiply_reduce_fusion
  465.6 3.7 fusion.34
  469.3 18.3 %multiply_subtract_fusion = f32[4,512,512]{2,1,0:T(8,128)} fusion(f32[4,512,512]{2,1,0:T(8,128)} %fusion.34, f32[512,512]{1,0:T(8,128)} %get-tuple-element.16, f32[512,512]{1,0:T(8,128)} %get-tuple-element.17, f32[4]{0:T(128)S(1)} %get-tuple-element.13, f32[512,512]{1,0:T(8,128)} %fusion.38, f32[4]{0:T(128)S(1)} %broadcast_multiply_fusion, ...), kind=kOutput, calls=%fused_computation.12 | convolution fusion | flops 2175795200 | bytes 15728672 | tf_op jit(solution)/shard_map/kij,kjl->kil/dot_general | solution.py:22
  487.6 6.1 %fusion.30 = bf16[4,512,512]{2,1,0:T(8,128)(2,1)} fusion(f32[4,512,512]{2,1,0:T(8,128)} %multiply_subtract_fusion), kind=kOutput, calls=%fused_computation.40 | convolution fusion | flops 1074790400 | bytes 6291456 | tf_op jit(solution)/shard_map/kij,kjl->kil/dot_general | solution.py:22
  493.7 11.2 %multiply_convert_fusion.1 = bf16[4,512,512]{2,1,0:T(8,128)(2,1)} fusion(f32[4,512,512]{2,1,0:T(8,128)} %multiply_subtract_fusion, f32[4]{0:T(128)S(1)} %get-tuple-element.12, bf16[4,512,512]{2,1,0:T(8,128)(2,1)} %fusion.30, f32[2,512,512]{2,1,0:T(8,128)S(1)} %bitcast_add_fusion, f32[2,512,512]{2,1,0:T(8,128)} %copy-done.2, f32[4]{0:T(128)S(1)} %get-tuple-element.13, ...), kind=kOutput, calls=%fused_computation.11 | convolution fusion | flops 3234856960 | bytes 13631536 | tf_op jit(solution)/shard_map/kij,kjl->kil/dot_general | solution.py:22
  504.9 2.1 convolution_convert_fusion.1
  507.0 1.0 multiply_reduce_fusion.2
  508.0 0.4 divide_convert_fusion
  508.4 1.3 copy.18
  509.7 53.6 %reduce-scatter.3.cloned.1.call-done = bf16[1024,256]{1,0:T(8,128)(2,1)} async-done(((bf16[1024,4096]{1,0:T(8,128)(2,1)}), bf16[1024,256]{1,0:T(8,128)(2,1)}) %reduce-scatter.3.cloned.1.call-update) | async-done | bytes 524304 | tf_op jit(solution)/shard_map/reduce_scatter | solution.py:66
  (20 shorter events, 0.1 us)
Async XLA Ops:
  7.2 173.3 %all-gather.5.cloned.1.call-start = ((), (), s32[]{:S(2)}) async-start(), calls=%async_computation.3 | async-start | bytes 9437184 | tf_op jit(solution)/shard_map/all_gather | solution.py:53
  7.9 252.9 %all-gather.3.cloned.1.call-start = ((), (), s32[]{:S(2)}) async-start(), calls=%async_computation.2 | async-start | bytes 8912896 | tf_op jit(solution)/shard_map/all_gather | solution.py:51
  8.6 266.9 %copy-start.5 = (bf16[1024,1024]{1,0:T(8,128)(2,1)S(1)}, bf16[1024,1024]{1,0:T(8,128)(2,1)}, u32[]{:S(2)}) copy-start(bf16[1024,1024]{1,0:T(8,128)(2,1)} %param.7) | copy-start | bytes 6291460
  8.7 446.7 %reduce-scatter.5.cloned.1.call-start = ((), (), s32[]{:S(2)}) async-start(), calls=%async_computation.5 | async-start | bytes 9437184 | tf_op jit(solution)/shard_map/reduce_scatter | solution.py:77
  260.8 14.7 %copy-start.4 = (bf16[1024,4096]{1,0:T(8,128)(2,1)S(1)}, bf16[1024,4096]{1,0:T(8,128)(2,1)}, u32[]{:S(2)}) copy-start(bf16[1024,4096]{1,0:T(8,128)(2,1)} %all-gather.3.cloned.1.call-done) | copy-start | bytes 25165828
  273.6 2.0 copy-start.7
  288.4 274.9 %reduce-scatter.3.cloned.1.call-start = ((), (), s32[]{:S(2)}) async-start(), calls=%async_computation.4 | async-start | bytes 8912896 | tf_op jit(solution)/shard_map/reduce_scatter | solution.py:66
  455.3 4.8 copy-start
  460.1 33.6 %copy-start.1 = (f32[2,512,512]{2,1,0:T(8,128)}, f32[2,512,512]{2,1,0:T(8,128)S(1)}, u32[]{:S(2)}) copy-start(f32[2,512,512]{2,1,0:T(8,128)S(1)} %bitcast_add_fusion) | copy-start | bytes 6291460
  460.1 3.2 copy-start.3
  463.3 2.2 copy-start.2
  504.9 2.1 copy-start.6
Sparse Core Ops, SparseCore 0:
  9.6 170.7 all-gather.4
  182.8 78.0 all-gather.2
  288.6 166.7 reduce-scatter.4
  460.0 103.2 reduce-scatter.2

commit v2 on v0

v2 whole, which is shorter than its diff:
```python
import jax
import jax.numpy as jnp
from jax import lax
from jax.experimental import pallas as pl
from jax.experimental.pallas import tpu as pltpu
from jax.sharding import PartitionSpec as P

MESH = pl.DeviceIdType.MESH
F32 = jnp.float32
BF16 = jnp.bfloat16

TOK = 1024
D = 4096
BLK = 512
COLS = 1024
FEAT = 256

decay_rate = 0.5
ridge_share = 0.05
epsilon = 1e-06
grad_scale = float(8192) ** (-0.5)

XA = (0, 192)
ZA = (192, 64)
ZB = (256, 64)
XB = (320, 192)
ZZ = (192, 128)
HA = (0, 256)
HB = (256, 256)
NSEM = 160


def dot(a, b):
    return jnp.dot(a, b, preferred_element_type=F32)


def gelu_slope(values):
    return (
        0.5 * (1.0 + lax.erf(values * 0.7071067811865476))
        + values * jnp.exp(-0.5 * values * values) * 0.3989422804014327
    )


def add_rows(dst, sources, rows, chunk=32):
    def body(i, carry):
        at = pl.ds(pl.multiple_of(i * chunk, chunk), chunk)
        total = sources[0][at, :].astype(F32)
        for source in sources[1:]:
            total = total + source[at, :].astype(F32)
        dst[at, :] = total.astype(dst.dtype)
        return carry

    lax.fori_loop(0, rows // chunk, body, 0)


def exchange_kernel(
    tok_ref, w_ref, cot_ref, tg_ref, gt_ref,
    wf, tok, hg, hgt, hid, part,
    s1, s1z, s2, s2z, rz, rx, sib, t1, t2, tx,
    ss, rs, ls,
):
    dp = lax.axis_index("dp")
    tn = lax.axis_index("tensor")
    c = lax.axis_index("pre")
    z, l = lax.div(dp, 2), lax.rem(dp, 2)
    xh, y = lax.div(tn, 4), lax.rem(tn, 4)
    m = 1 - l
    up, um, u2 = lax.rem(z + 1, 4), lax.rem(z + 3, 4), lax.rem(z + 2, 4)
    yp, ym, y2 = lax.rem(y + 1, 4), lax.rem(y + 3, 4), lax.rem(y + 2, 4)
    oh, oc = 1 - xh, 1 - c
    dev_zp, dev_zm = (up * 2 + l, tn, c), (um * 2 + l, tn, c)
    dev_x = (z * 2 + m, tn, c)
    dev_yp, dev_ym = (dp, xh * 4 + yp, c), (dp, xh * 4 + ym, c)
    dev_h = (dp, oh * 4 + y, c)
    dev_c = (dp, tn, oc)

    barrier = pltpu.get_barrier_semaphore()
    for dev in (dev_zp, dev_zm, dev_x, dev_yp, dev_ym, dev_h, dev_c):
        pl.semaphore_signal(barrier, inc=1, device_id=dev, device_id_type=MESH)
    pl.semaphore_wait(barrier, 7)

    copies = []

    def send(src, dst, dev):
        k = len(copies)
        copy = pltpu.make_async_remote_copy(
            src_ref=src, dst_ref=dst, send_sem=ss.at[k], recv_sem=rs.at[k],
            device_id=dev, device_id_type=MESH,
        )
        copy.start()
        copies.append(copy)
        return copy

    def got(*several):
        for copy in several:
            copy.wait_recv()

    def rows_of(zi, li, rows):
        return pl.ds(pl.multiple_of((zi * 2 + li) * BLK + rows[0], 64), rows[1])

    def wpart(zi, li, rows, h):
        return wf.at[rows_of(zi, li, rows), pl.ds(h * BLK, BLK)]

    def wsend(zi, li, rows, h, dev):
        ref = wpart(zi, li, rows, h)
        return send(ref, ref, dev)

    wstate = [dict(), dict()]

    def w_own(h):
        q = wstate[h]

        def own(rows, dev):
            return send(
                w_ref.at[pl.ds(rows[0], rows[1]), pl.ds(h * BLK, BLK)],
                wpart(z, l, rows, h), dev,
            )

        q["xa"], q["xb"] = own(XA, dev_x), own(XB, dev_x)
        q["pa"], q["mb"] = own(HA, dev_zp), own(HB, dev_zm)
        q["pb"], q["ma"] = own(HB, dev_zp), own(HA, dev_zm)
        q["xz"] = own(ZZ, dev_x)

    def w_partner(h):
        q = wstate[h]
        got(q["xa"])
        q["ppa"] = wsend(z, m, XA, h, dev_zp)
        q["pma"] = wsend(z, m, XA, h, dev_zm)
        got(q["xb"])
        q["pmb"] = wsend(z, m, XB, h, dev_zm)
        q["ppb"] = wsend(z, m, XB, h, dev_zp)

    def w_forward_own(h):
        q = wstate[h]
        got(q["pa"])
        q["fa"] = wsend(um, l, HA, h, dev_zp)
        got(q["mb"])
        q["fb"] = wsend(up, l, HB, h, dev_zm)
        got(q["pb"])
        q["xzm"] = wsend(um, l, ZZ, h, dev_x)
        got(q["ma"])
        q["xzp"] = wsend(up, l, ZZ, h, dev_x)

    def w_forward_partner(h):
        q = wstate[h]
        got(q["ppa"])
        q["fpa"] = wsend(um, m, XA, h, dev_zp)
        got(q["pmb"])
        q["fpb"] = wsend(up, m, XB, h, dev_zm)

    def w_last(h):
        q = wstate[h]
        got(q["fa"])
        q["x2a"] = wsend(u2, l, ZA, h, dev_x)
        got(q["fb"])
        q["x2b"] = wsend(u2, l, ZB, h, dev_x)

    def w_done(h):
        q = wstate[h]
        got(*(q[k] for k in ("xz", "ppb", "pma", "xzm", "xzp", "fpa", "fpb", "x2a", "x2b")))

    TA, TB = pl.ds(0, TOK // 2), pl.ds(TOK // 2, TOK // 2)
    ALL = pl.ds(0, TOK)

    def tcols(hi, yi, ci):
        return pl.ds(pl.multiple_of(((hi * 4 + yi) * 2 + ci) * FEAT, FEAT), FEAT)

    def tsend(hi, yi, rows, dev):
        ref = tok.at[rows, tcols(hi, yi, c)]
        return send(ref, ref, dev)

    tq = {}

    def t_own():
        def own(rows, dev):
            return send(tok_ref.at[rows, :], tok.at[rows, tcols(xh, y, c)], dev)

        tq["h"] = own(ALL, dev_h)
        tq["pa"], tq["mb"] = own(TA, dev_yp), own(TB, dev_ym)
        tq["pb"], tq["ma"] = own(TB, dev_yp), own(TA, dev_ym)
        tq["c0"] = own(ALL, dev_c)

    def t_partner():
        got(tq["h"])
        tq["hpa"], tq["hmb"] = tsend(oh, y, TA, dev_yp), tsend(oh, y, TB, dev_ym)
        tq["hpb"], tq["hma"] = tsend(oh, y, TB, dev_yp), tsend(oh, y, TA, dev_ym)
        tq["c1"] = tsend(oh, y, ALL, dev_c)

    def t_forward_own():
        got(tq["pa"])
        tq["fa"] = tsend(xh, ym, TA, dev_yp)
        got(tq["mb"])
        tq["fb"] = tsend(xh, yp, TB, dev_ym)
        got(tq["pb"])
        tq["c2"] = tsend(xh, ym, ALL, dev_c)
        got(tq["ma"])
        tq["c3"] = tsend(xh, yp, ALL, dev_c)

    def t_forward_partner():
        got(tq["hpa"])
        tq["hfa"] = tsend(oh, ym, TA, dev_yp)
        got(tq["hmb"])
        tq["hfb"] = tsend(oh, yp, TB, dev_ym)
        got(tq["hpb"])
        tq["c4"] = tsend(oh, ym, ALL, dev_c)
        got(tq["hma"])
        tq["c5"] = tsend(oh, yp, ALL, dev_c)

    def t_last():
        got(tq["fa"], tq["fb"])
        tq["c6"] = tsend(xh, y2, ALL, dev_c)
        got(tq["hfa"], tq["hfb"])
        tq["c7"] = tsend(oh, y2, ALL, dev_c)

    def t_done():
        got(*(tq["c%d" % i] for i in range(8)))

    def hidden(h):
        cols = pl.ds(h * BLK, BLK)

        def tile(i, carry):
            at = pl.ds(pl.multiple_of(i * 256, 256), 256)
            hid[...] = dot(tok[at, :], wf[:, cols])

            def slope(j, inner):
                small = pl.ds(pl.multiple_of(j * 16, 16), 16)
                big = pl.ds(pl.multiple_of(i * 256 + j * 16, 16), 16)
                cot = hg[big, cols].astype(F32)
                hg[big, cols] = (cot * gelu_slope(hid[small, :])).astype(BF16)
                return inner

            lax.fori_loop(0, 16, slope, 0)
            return carry

        lax.fori_loop(0, TOK // 256, tile, 0)

    def gradient(h):
        cols = pl.ds(h * BLK, BLK)
        for i in range(4):
            at = pl.ds(i * 256, 256)
            hgt[:, at] = hg[at, cols].T

        def block(d, carry):
            at = pl.ds(pl.multiple_of(d * BLK, BLK), BLK)
            part[h, d] = (dot(hgt[...], tok[:, at]) * grad_scale).astype(BF16)
            return carry

        lax.fori_loop(0, 8, block, 0)

    def input_part():
        def block(n, carry):
            at = pl.ds(pl.multiple_of(n * BLK, BLK), BLK)
            tok[:, at] = lax.dot_general(
                hg[...], wf[at, :], (((1,), (1,)), ((), ())), preferred_element_type=F32
            ).astype(BF16)
            return carry

        lax.fori_loop(0, 8, block, 0)

    def ppart(h, zi, li, rows):
        return part.at[h, zi * 2 + li, pl.ds(rows[0], rows[1]), :]

    gstate = [dict(), dict()]
    OTHER, OWN = 0, 1
    DN, UP = 0, 1

    def g_start(h):
        q = gstate[h]
        for zi, name in ((u2, "rz2"), (up, "rzp"), (um, "rzm"), (z, "rz0")):
            q[name] = send(ppart(h, zi, m, ZZ), rz.at[h, zi], dev_x)
        for side, li in ((OTHER, m), (OWN, l)):
            q["1p", side] = send(ppart(h, u2, li, XA), s1.at[h, UP, side], dev_zp)
            q["1m", side] = send(ppart(h, u2, li, XB), s1.at[h, DN, side], dev_zm)
        for side, li in ((OTHER, m), (OWN, l)):
            q["2pb", side] = send(ppart(h, up, li, XB), s2.at[h, UP, side, 1], dev_zp)
            q["2ma", side] = send(ppart(h, um, li, XA), s2.at[h, DN, side, 0], dev_zm)

    def g_second(h):
        q = gstate[h]
        for side, li in ((OTHER, m), (OWN, l)):
            got(q["1p", side])
            mine = ppart(h, up, li, XA)
            add_rows(mine, (mine, s1.at[h, UP, side]), XA[1])
            q["2pa", side] = send(mine, s2.at[h, UP, side, 0], dev_zp)
            got(q["1m", side])
            mine = ppart(h, um, li, XB)
            add_rows(mine, (mine, s1.at[h, DN, side]), XB[1])
            q["2mb", side] = send(mine, s2.at[h, DN, side, 1], dev_zm)

    def g_middle(h):
        q = gstate[h]
        for zi, name in ((u2, "rz2"), (up, "rzp"), (um, "rzm"), (z, "rz0")):
            got(q[name])
            mine = ppart(h, zi, l, ZZ)
            add_rows(mine, (mine, rz.at[h, zi]), ZZ[1])
        q["z1p"] = send(ppart(h, u2, l, ZA), s1z.at[h, UP], dev_zp)
        q["z1m"] = send(ppart(h, u2, l, ZB), s1z.at[h, DN], dev_zm)
        q["z2pb"] = send(ppart(h, up, l, ZB), s2z.at[h, UP, 1], dev_zp)
        q["z2ma"] = send(ppart(h, um, l, ZA), s2z.at[h, DN, 0], dev_zm)

    def g_middle_second(h):
        q = gstate[h]
        got(q["z1p"])
        mine = ppart(h, up, l, ZA)
        add_rows(mine, (mine, s1z.at[h, UP]), ZA[1])
        q["z2pa"] = send(mine, s2z.at[h, UP, 0], dev_zp)
        got(q["z1m"])
        mine = ppart(h, um, l, ZB)
        add_rows(mine, (mine, s1z.at[h, DN]), ZB[1])
        q["z2mb"] = send(mine, s2z.at[h, DN, 1], dev_zm)

    def g_cross(h):
        q = gstate[h]
        for k, rows, name in ((0, XA, "a"), (1, XB, "b")):
            got(q["2p" + name, OTHER], q["2m" + name, OTHER])
            mine = ppart(h, z, m, rows)
            add_rows(mine, (mine, s2.at[h, UP, OTHER, k], s2.at[h, DN, OTHER, k]), rows[1])
            q["x" + name] = send(mine, rx.at[h, k], dev_x)

    def g_final(h):
        q = gstate[h]
        for k, rows, name in ((0, ZA, "a"), (1, ZB, "b")):
            got(q["z2p" + name], q["z2m" + name])
            add_rows(
                gt_ref.at[h, pl.ds(rows[0], rows[1]), :],
                (ppart(h, z, l, rows), s2z.at[h, UP, k], s2z.at[h, DN, k]),
                rows[1],
            )
        for k, rows, name in ((0, XA, "a"), (1, XB, "b")):
            got(q["2p" + name, OWN], q["2m" + name, OWN], q["x" + name])
            add_rows(
                gt_ref.at[h, pl.ds(rows[0], rows[1]), :],
                (ppart(h, z, l, rows), s2.at[h, UP, OWN, k], s2.at[h, DN, OWN, k], rx.at[h, k]),
                rows[1],
            )

    dq = {}

    def dpart(hi, yi, ci, rows):
        return tok.at[rows, tcols(hi, yi, ci)]

    sides = ((OTHER, oh), (OWN, xh))

    def d_start():
        for yi, name in ((y2, "2"), (yp, "p"), (ym, "m"), (y, "0")):
            for side, hi in sides:
                dq["c" + name, side] = send(
                    dpart(hi, yi, oc, ALL), sib.at[hi * 4 + yi], dev_c
                )

    def d_add(name, yi):
        for side, hi in sides:
            got(dq["c" + name, side])
            mine = dpart(hi, yi, c, ALL)
            add_rows(mine, (mine, sib.at[hi * 4 + yi]), TOK)

    def d_first():
        d_add("2", y2)
        for side, hi in sides:
            dq["1p", side] = send(dpart(hi, y2, c, TA), t1.at[UP, side], dev_yp)
            dq["1m", side] = send(dpart(hi, y2, c, TB), t1.at[DN, side], dev_ym)
        d_add("p", yp)
        for side, hi in sides:
            dq["2pb", side] = send(dpart(hi, yp, c, TB), t2.at[UP, side, 1], dev_yp)
        d_add("m", ym)
        for side, hi in sides:
            dq["2ma", side] = send(dpart(hi, ym, c, TA), t2.at[DN, side, 0], dev_ym)
        d_add("0", y)

    def d_second():
        for side, hi in sides:
            got(dq["1p", side])
            mine = dpart(hi, yp, c, TA)
            add_rows(mine, (mine, t1.at[UP, side]), TOK // 2)
            dq["2pa", side] = send(mine, t2.at[UP, side, 0], dev_yp)
            got(dq["1m", side])
            mine = dpart(hi, ym, c, TB)
            add_rows(mine, (mine, t1.at[DN, side]), TOK // 2)
            dq["2mb", side] = send(mine, t2.at[DN, side, 1], dev_ym)

    def d_cross():
        for k, rows, name in ((0, TA, "a"), (1, TB, "b")):
            got(dq["2p" + name, OTHER], dq["2m" + name, OTHER])
            mine = dpart(oh, y, c, rows)
            add_rows(mine, (mine, t2.at[UP, OTHER, k], t2.at[DN, OTHER, k]), TOK // 2)
            dq["x" + name] = send(mine, tx.at[k], dev_h)

    def d_final():
        for k, rows, name in ((0, TA, "a"), (1, TB, "b")):
            got(dq["2p" + name, OWN], dq["2m" + name, OWN], dq["x" + name])
            add_rows(
                tg_ref.at[rows, :],
                (dpart(xh, y, c, rows), t2.at[UP, OWN, k], t2.at[DN, OWN, k], tx.at[k]),
                TOK // 2,
            )

    local = [
        pltpu.make_async_copy(w_ref, wf.at[rows_of(z, l, (0, BLK)), :], ls.at[0]),
        pltpu.make_async_copy(tok_ref, tok.at[:, tcols(xh, y, c)], ls.at[1]),
        pltpu.make_async_copy(cot_ref, hg, ls.at[2]),
    ]
    w_own(0)
    t_own()
    for copy in local:
        copy.start()
    t_partner()
    w_partner(0)
    t_forward_own()
    w_forward_own(0)
    t_forward_partner()
    w_forward_partner(0)
    w_own(1)
    t_last()
    w_last(0)
    for copy in local:
        copy.wait()
    t_done()
    w_done(0)
    w_partner(1)
    hidden(0)
    w_forward_own(1)
    gradient(0)
    g_start(0)
    w_forward_partner(1)
    w_last(1)
    g_second(0)
    g_middle(0)
    w_done(1)
    hidden(1)
    g_middle_second(0)
    gradient(1)
    g_start(1)
    g_cross(0)
    for copy in tq.values():
        copy.wait_send()
    input_part()
    d_start()
    g_second(1)
    d_first()
    g_middle(1)
    g_final(0)
    d_second()
    g_middle_second(1)
    d_cross()
    g_cross(1)
    d_final()
    g_final(1)
    waited = [id(copy) for copy in tq.values()]
    for copy in copies:
        if id(copy) not in waited:
            copy.wait_send()


def exchange(tokens, weight, cotangent):
    any_spec = pl.BlockSpec(memory_space=pl.ANY)
    vmem_spec = pl.BlockSpec(memory_space=pltpu.VMEM)
    dma = pltpu.SemaphoreType.DMA
    return pl.pallas_call(
        exchange_kernel,
        out_shape=(
            jax.ShapeDtypeStruct((TOK, FEAT), BF16),
            jax.ShapeDtypeStruct((2, BLK, BLK), F32),
        ),
        in_specs=[any_spec, any_spec, any_spec],
        out_specs=(vmem_spec, vmem_spec),
        scratch_shapes=[
            pltpu.VMEM((D, COLS), BF16),
            pltpu.VMEM((TOK, D), BF16),
            pltpu.VMEM((TOK, COLS), BF16),
            pltpu.VMEM((BLK, TOK), BF16),
            pltpu.VMEM((256, BLK), F32),
            pltpu.VMEM((2, 8, BLK, BLK), BF16),
            pltpu.VMEM((2, 2, 2, XA[1], BLK), BF16),
            pltpu.VMEM((2, 2, ZA[1], BLK), BF16),
            pltpu.VMEM((2, 2, 2, 2, XA[1], BLK), BF16),
            pltpu.VMEM((2, 2, 2, ZA[1], BLK), BF16),
            pltpu.VMEM((2, 4, ZZ[1], BLK), BF16),
            pltpu.VMEM((2, 2, XA[1], BLK), BF16),
            pltpu.VMEM((8, TOK, FEAT), BF16),
            pltpu.VMEM((2, 2, TOK // 2, FEAT), BF16),
            pltpu.VMEM((2, 2, 2, TOK // 2, FEAT), BF16),
            pltpu.VMEM((2, TOK // 2, FEAT), BF16),
            dma((NSEM,)),
            dma((NSEM,)),
            dma((3,)),
        ],
        compiler_params=pltpu.CompilerParams(
            collective_id=0, has_side_effects=True, vmem_limit_bytes=60 * 2**20
        ),
        cost_estimate=pl.CostEstimate(
            flops=6 * TOK * D * COLS, bytes_accessed=2**24, transcendentals=2 * TOK * COLS
        ),
        name="exchange",
    )(tokens, weight, cotangent)


def total_of(values):
    return jnp.sum(jnp.sum(values, axis=1, keepdims=True), axis=0, keepdims=True)


def precondition_kernel(gt_ref, left_ref, right_ref, update_ref, left_out, right_out):
    gt = gt_ref[0]
    grad = gt.T
    gth, gh = gt.astype(BF16), grad.astype(BF16)
    rows = lax.broadcasted_iota(jnp.int32, (BLK, BLK), 0)
    cols = lax.broadcasted_iota(jnp.int32, (BLK, BLK), 1)
    eye = jnp.where(rows == cols, 1.0, 0.0).astype(F32)
    share = (1.0 - decay_rate) / BLK
    left = decay_rate * left_ref[0, 0] + share * dot(gh, gth)
    right = decay_rate * right_ref[0, 0] + share * dot(gth, gh)
    left_out[0, 0] = left
    right_out[0, 0] = right

    def each(function, *lists):
        return [function(*items) for items in zip(*lists)]

    def start(stat):
        trace = total_of(stat * eye)
        regular = stat + (ridge_share * trace / BLK) * eye
        scale = jnp.sqrt(total_of(regular * regular)) / 4.0
        return regular / scale, scale

    begun = each(start, (left, right))
    first = [b[0] for b in begun]
    scales = [b[1] for b in begun]
    firsth = each(lambda a: a.astype(BF16), first)
    square = each(dot, firsth, firsth)
    zero_sq = each(
        lambda a, q: (1.5625 * eye - 0.625 * a + 0.0625 * q).astype(BF16), first, square
    )
    crossed = each(lambda a, q: (1.25 * a - 0.25 * q).astype(BF16), first, square)
    fourth = each(lambda a: dot(a, a).astype(BF16), zero_sq)
    two = each(
        lambda a, f, x: 1.5625 * eye - 0.3125 * a - 0.25 * dot(f, x), first, fourth, crossed
    )
    twoh = each(lambda a: a.astype(BF16), two)
    two_sq = each(lambda a: dot(a, a).astype(BF16), twoh)
    two_crossed = each(lambda a, f: dot(a, f).astype(BF16), twoh, firsth)
    two_fourth = each(lambda a: dot(a, a).astype(BF16), two_sq)
    roots = each(
        lambda a, f, x, s: (
            lax.rsqrt(jnp.sqrt(s)) * (1.25 * a - 0.25 * dot(f, x))
        ).astype(BF16),
        two, two_fourth, two_crossed, scales,
    )
    left_part = dot(roots[0], gh).astype(BF16)
    raw = dot(left_part, roots[1])
    size = float(BLK * BLK)
    grad_rms = jnp.sqrt(total_of(gt * gt) / size)
    raw_rms = jnp.sqrt(total_of(raw * raw) / size + epsilon)
    update_ref[...] = (raw * (grad_rms / raw_rms)).astype(BF16)


def precondition(gt, left_stats, right_stats):
    stat_spec = pl.BlockSpec((1, 1, BLK, BLK), lambda h: (0, h, 0, 0))
    return pl.pallas_call(
        precondition_kernel,
        grid=(2,),
        out_shape=(
            jax.ShapeDtypeStruct((BLK, COLS), BF16),
            jax.ShapeDtypeStruct(left_stats.shape, F32),
            jax.ShapeDtypeStruct(right_stats.shape, F32),
        ),
        in_specs=[pl.BlockSpec((1, BLK, BLK), lambda h: (h, 0, 0)), stat_spec, stat_spec],
        out_specs=(pl.BlockSpec((BLK, BLK), lambda h: (0, h)), stat_spec, stat_spec),
        compiler_params=pltpu.CompilerParams(vmem_limit_bytes=56 * 2**20),
        name="precondition",
    )(gt, left_stats, right_stats)


def shards(tokens, weight, cotangent, left_stats, right_stats):
    tokens_grad, gt = exchange(tokens, weight, cotangent)
    update, left_new, right_new = precondition(gt, left_stats, right_stats)
    return tokens_grad, update, left_new, right_new


def solution(mesh):
    two = P("dp", ("tensor", "pre"))
    four = P("dp", ("tensor", "pre"), None, None)
    return jax.shard_map(
        shards,
        mesh=mesh,
        in_specs=(two, two, two, four, four),
        out_specs=(two, two, four, four),
        check_vma=False,
    )
```

time: 576 us -> 202 us (0.35)
  waiting for transfers between devices: 435 us -> 0 us
  Pallas kernels: 0 us -> 199 us
  matrix products: 109 us -> 0 us
  between operations: 14.2 us -> 0.65 us
  other arithmetic: 6.35 us -> 0 us
    all_gather x2 -> x0, waiting for transfers between devices: 252 us -> none  [the longest x1 172 us: shards(): lax.all_gather(weight, 'dp', axis=0, tiled=True)]
    pallas_call x0 -> x2, Pallas kernels: none -> 199 us  [the longest x1 184 us: exchange(): pl.pallas_call(exchange_kernel, out_shape=(jax.ShapeDtypeStruct((TOK, FEA...]
    reduce_scatter x2 -> x0, waiting for transfers between devices: 182 us -> none  [the longest x1 148 us: shards(): lax.psum_scatter(grad_part.astype(jnp.bfloat16), 'dp', scatter_dimension=...]
    dot_general x15 -> x0, matrix products: 109 us -> none  [the longest x8 62.7 us: matmul_high(): jnp.einsum('kij,kjl->kil', left, right, precision=lax.Precision.HIGHEST)]
  transfers between devices with their start and end apart: 4 -> 0, of which waited for: 4 -> 0; matrix products, arithmetic and copies ran while one was open for 16% -> 0% of each run, Pallas kernels for 0% -> 0%
where the time goes in v2:
time: 202 us; the launch traced here: 200 us
  Pallas kernels  199 us (99%)
    pallas_call x1, Pallas kernels, exchange(): pl.pallas_call(exchange_kernel, out_shape=(jax.ShapeDtypeStruct((TOK, FEA...  184 us
    pallas_call x1, Pallas kernels, precondition(): pl.pallas_call(precondition_kernel, grid=(2,), out_shape=(jax.ShapeDtypeS...  15.3 us

profile of v2, /device:TPU:0, one launch (start us, length us, event | category | flops | bytes accessed | tf_op | source)
XLA Modules:
  0.0 200.4 jit_solution(7636233558473691546)
XLA Ops:
  0.6 183.6 %exchange.1 = (bf16[1024,256]{1,0:T(8,128)(2,1)}, f32[2,512,512]{2,1,0:T(8,128)}) custom-call(bf16[1024,256]{1,0:T(8,128)(2,1)} %tok_ref.1, bf16[512,1024]{1,0:T(8,128)(2,1)} %w_ref.1, bf16[1024,1024]{1,0:T(8,128)(2,1)} %cot_ref.1), custom_call_target="tpu_custom_call" | custom-call | flops 25769803776 | bytes 16777216 | tf_op jit(solution)/shard_map/exchange/pallas_call | solution.py:458
  184.2 0.0 copy-start
  184.2 15.3 %precondition.1 = (bf16[512,1024]{1,0:T(8,128)(2,1)}, f32[1,2,512,512]{3,2,1,0:T(8,128)}, f32[1,2,512,512]{3,2,1,0:T(8,128)}) custom-call(f32[2,512,512]{2,1,0:T(8,128)} %get-tuple-element.10.gt_ref, f32[1,2,512,512]{3,2,1,0:T(8,128)} %left_ref.1, f32[1,2,512,512]{3,2,1,0:T(8,128)} %right_ref.1), custom_call_target="tpu_custom_call" | custom-call | tf_op jit(solution)/shard_map/precondition/pallas_call | solution.py:556
  199.6 0.0 copy-done
  199.6 0.8 copy.10
Async XLA Ops:
  184.2 15.4 %copy-start = (bf16[1024,256]{1,0:T(8,128)(2,1)S(1)}, bf16[1024,256]{1,0:T(8,128)(2,1)}, u32[]{:S(2)}) copy-start(bf16[1024,256]{1,0:T(8,128)(2,1)} %get-tuple-element.18) | copy-start | bytes 1572868

commit v3 on v2

--- a/solution.py
+++ b/solution.py
@@ -20,11 +20,11 @@
 epsilon = 1e-06
 grad_scale = float(8192) ** (-0.5)
 
-XA = (0, 192)
-ZA = (192, 64)
-ZB = (256, 64)
-XB = (320, 192)
-ZZ = (192, 128)
+XA = (0, 176)
+ZA = (176, 80)
+ZB = (256, 80)
+XB = (336, 176)
+ZZ = (176, 160)
 HA = (0, 256)
 HB = (256, 256)
 NSEM = 160
@@ -41,7 +41,7 @@
     )
 
 
-def add_rows(dst, sources, rows, chunk=32):
+def add_rows(dst, sources, rows, chunk=16):
     def body(i, carry):
         at = pl.ds(pl.multiple_of(i * chunk, chunk), chunk)
         total = sources[0][at, :].astype(F32)
@@ -55,7 +55,7 @@
 
 def exchange_kernel(
     tok_ref, w_ref, cot_ref, tg_ref, gt_ref,
-    wf, tok, hg, hgt, hid, part,
+    wf, tok, hg, hgt, hid, part, dout,
     s1, s1z, s2, s2z, rz, rx, sib, t1, t2, tx,
     ss, rs, ls,
 ):
@@ -96,7 +96,7 @@
             copy.wait_recv()
 
     def rows_of(zi, li, rows):
-        return pl.ds(pl.multiple_of((zi * 2 + li) * BLK + rows[0], 64), rows[1])
+        return pl.ds(pl.multiple_of((zi * 2 + li) * BLK + rows[0], 16), rows[1])
 
     def wpart(zi, li, rows, h):
         return wf.at[rows_of(zi, li, rows), pl.ds(h * BLK, BLK)]
@@ -107,7 +107,7 @@
 
     wstate = [dict(), dict()]
 
-    def w_own(h):
+    def w_own(h, first):
         q = wstate[h]
 
         def own(rows, dev):
@@ -116,19 +116,21 @@
                 wpart(z, l, rows, h), dev,
             )
 
-        q["xa"], q["xb"] = own(XA, dev_x), own(XB, dev_x)
-        q["pa"], q["mb"] = own(HA, dev_zp), own(HB, dev_zm)
-        q["pb"], q["ma"] = own(HB, dev_zp), own(HA, dev_zm)
-        q["xz"] = own(ZZ, dev_x)
+        if first:
+            q["pa"], q["mb"] = own(HA, dev_zp), own(HB, dev_zm)
+            q["xa"], q["xb"] = own(XA, dev_x), own(XB, dev_x)
+        else:
+            q["pb"], q["ma"] = own(HB, dev_zp), own(HA, dev_zm)
+            q["xz"] = own(ZZ, dev_x)
 
     def w_partner(h):
         q = wstate[h]
         got(q["xa"])
         q["ppa"] = wsend(z, m, XA, h, dev_zp)
-        q["pma"] = wsend(z, m, XA, h, dev_zm)
         got(q["xb"])
         q["pmb"] = wsend(z, m, XB, h, dev_zm)
         q["ppb"] = wsend(z, m, XB, h, dev_zp)
+        q["pma"] = wsend(z, m, XA, h, dev_zm)
 
     def w_forward_own(h):
         q = wstate[h]
@@ -136,6 +138,9 @@
         q["fa"] = wsend(um, l, HA, h, dev_zp)
         got(q["mb"])
         q["fb"] = wsend(up, l, HB, h, dev_zm)
+
+    def w_cross(h):
+        q = wstate[h]
         got(q["pb"])
         q["xzm"] = wsend(um, l, ZZ, h, dev_x)
         got(q["ma"])
@@ -191,6 +196,8 @@
         tq["fa"] = tsend(xh, ym, TA, dev_yp)
         got(tq["mb"])
         tq["fb"] = tsend(xh, yp, TB, dev_ym)
+
+    def t_share_own():
         got(tq["pb"])
         tq["c2"] = tsend(xh, ym, ALL, dev_c)
         got(tq["ma"])
@@ -206,16 +213,20 @@
         got(tq["hma"])
         tq["c5"] = tsend(oh, yp, ALL, dev_c)
 
-    def t_last():
+    def t_last_own():
         got(tq["fa"], tq["fb"])
         tq["c6"] = tsend(xh, y2, ALL, dev_c)
+
+    def t_last():
         got(tq["hfa"], tq["hfb"])
         tq["c7"] = tsend(oh, y2, ALL, dev_c)
 
     def t_done():
         got(*(tq["c%d" % i] for i in range(8)))
 
-    def hidden(h):
+    dq = {}
+
+    def hidden(h, r):
         cols = pl.ds(h * BLK, BLK)
 
         def tile(i, carry):
@@ -232,7 +243,7 @@
             lax.fori_loop(0, 16, slope, 0)
             return carry
 
-        lax.fori_loop(0, TOK // 256, tile, 0)
+        lax.fori_loop(2 * r, 2 * r + 2, tile, 0)
 
     def gradient(h):
         cols = pl.ds(h * BLK, BLK)
@@ -247,12 +258,29 @@
 
         lax.fori_loop(0, 8, block, 0)
 
-    def input_part():
-        def block(n, carry):
-            at = pl.ds(pl.multiple_of(n * BLK, BLK), BLK)
-            tok[:, at] = lax.dot_general(
-                hg[...], wf[at, :], (((1,), (1,)), ((), ())), preferred_element_type=F32
-            ).astype(BF16)
+    def wide_dot(rows, g):
+        at = pl.ds(pl.multiple_of(g * FEAT, FEAT), FEAT)
+        return lax.dot_general(
+            hg[rows, :], wf[at, :], (((1,), (1,)), ((), ())), preferred_element_type=F32
+        )
+
+    def input_other(r):
+        rows = pl.ds(r * (TOK // 2), TOK // 2)
+
+        def block(t, carry):
+            dout[t, rows, :] = wide_dot(rows, t * 2 + oc).astype(BF16)
+            return carry
+
+        lax.fori_loop(0, 8, block, 0)
+        dq["c", r] = send(dout.at[:, rows, :], sib.at[:, rows, :], dev_c)
+
+    def input_own(r):
+        got(dq["c", r])
+        rows = pl.ds(r * (TOK // 2), TOK // 2)
+
+        def block(t, carry):
+            mine = wide_dot(rows, t * 2 + c) + sib[t, rows, :].astype(F32)
+            sib[t, rows, :] = mine.astype(BF16)
             return carry
 
         lax.fori_loop(0, 8, block, 0)
@@ -334,38 +362,19 @@
                 rows[1],
             )
 
-    dq = {}
-
     def dpart(hi, yi, ci, rows):
-        return tok.at[rows, tcols(hi, yi, ci)]
+        return sib.at[hi * 4 + yi, rows, :]
 
     sides = ((OTHER, oh), (OWN, xh))
 
-    def d_start():
-        for yi, name in ((y2, "2"), (yp, "p"), (ym, "m"), (y, "0")):
-            for side, hi in sides:
-                dq["c" + name, side] = send(
-                    dpart(hi, yi, oc, ALL), sib.at[hi * 4 + yi], dev_c
-                )
-
-    def d_add(name, yi):
+    def d_first(r):
         for side, hi in sides:
-            got(dq["c" + name, side])
-            mine = dpart(hi, yi, c, ALL)
-            add_rows(mine, (mine, sib.at[hi * 4 + yi]), TOK)
-
-    def d_first():
-        d_add("2", y2)
-        for side, hi in sides:
-            dq["1p", side] = send(dpart(hi, y2, c, TA), t1.at[UP, side], dev_yp)
-            dq["1m", side] = send(dpart(hi, y2, c, TB), t1.at[DN, side], dev_ym)
-        d_add("p", yp)
-        for side, hi in sides:
-            dq["2pb", side] = send(dpart(hi, yp, c, TB), t2.at[UP, side, 1], dev_yp)
-        d_add("m", ym)
-        for side, hi in sides:
-            dq["2ma", side] = send(dpart(hi, ym, c, TA), t2.at[DN, side, 0], dev_ym)
-        d_add("0", y)
+            if r == 0:
+                dq["1p", side] = send(dpart(hi, y2, c, TA), t1.at[UP, side], dev_yp)
+                dq["2ma", side] = send(dpart(hi, ym, c, TA), t2.at[DN, side, 0], dev_ym)
+            else:
+                dq["1m", side] = send(dpart(hi, y2, c, TB), t1.at[DN, side], dev_ym)
+                dq["2pb", side] = send(dpart(hi, yp, c, TB), t2.at[UP, side, 1], dev_yp)
 
     def d_second():
         for side, hi in sides:
@@ -399,56 +408,63 @@
         pltpu.make_async_copy(tok_ref, tok.at[:, tcols(xh, y, c)], ls.at[1]),
         pltpu.make_async_copy(cot_ref, hg, ls.at[2]),
     ]
-    w_own(0)
+    w_own(0, True)
+    w_own(0, False)
     t_own()
+    t_forward_own()
     for copy in local:
         copy.start()
+    w_forward_own(0)
+    w_own(1, True)
+    w_last(0)
+    w_partner(0)
+    w_cross(0)
     t_partner()
-    w_partner(0)
-    t_forward_own()
-    w_forward_own(0)
+    w_own(1, False)
+    w_forward_partner(0)
+    w_forward_own(1)
+    t_last_own()
+    w_partner(1)
     t_forward_partner()
-    w_forward_partner(0)
-    w_own(1)
+    t_share_own()
+    w_cross(1)
+    w_done(0)
     t_last()
-    w_last(0)
+    t_done()
     for copy in local:
         copy.wait()
-    t_done()
-    w_done(0)
-    w_partner(1)
-    hidden(0)
-    w_forward_own(1)
+    hidden(0, 1)
+    hidden(0, 0)
+    w_forward_partner(1)
+    w_last(1)
     gradient(0)
     g_start(0)
-    w_forward_partner(1)
-    w_last(1)
+    w_done(1)
+    hidden(1, 0)
+    hidden(1, 1)
+    input_other(0)
     g_second(0)
+    gradient(1)
+    input_own(0)
+    d_first(0)
+    g_start(1)
+    input_other(1)
+    input_own(1)
+    g_cross(0)
+    d_first(1)
+    g_second(1)
+    d_second()
+    g_cross(1)
     g_middle(0)
-    w_done(1)
-    hidden(1)
     g_middle_second(0)
-    gradient(1)
-    g_start(1)
-    g_cross(0)
-    for copy in tq.values():
-        copy.wait_send()
-    input_part()
-    d_start()
-    g_second(1)
-    d_first()
+    d_cross()
     g_middle(1)
     g_final(0)
-    d_second()
     g_middle_second(1)
-    d_cross()
-    g_cross(1)
+    g_final(1)
     d_final()
-    g_final(1)
-    waited = [id(copy) for copy in tq.values()]
     for copy in copies:
-        if id(copy) not in waited:
-            copy.wait_send()
+        copy.wait_send()
 
 
 def exchange(tokens, weight, cotangent):
@@ -470,6 +486,7 @@
             pltpu.VMEM((BLK, TOK), BF16),
             pltpu.VMEM((256, BLK), F32),
             pltpu.VMEM((2, 8, BLK, BLK), BF16),
+            pltpu.VMEM((8, TOK, FEAT), BF16),
             pltpu.VMEM((2, 2, 2, XA[1], BLK), BF16),
             pltpu.VMEM((2, 2, ZA[1], BLK), BF16),
             pltpu.VMEM((2, 2, 2, 2, XA[1], BLK), BF16),

time: 202 us -> 156 us (0.77)
  Pallas kernels: 199 us -> 154 us
    pallas_call x1, Pallas kernels: 184 us -> 138 us  [exchange(): pl.pallas_call(exchange_kernel, out_shape=(jax.ShapeDtypeStruct((TOK, FEA...]
where the time goes in v3:
time: 156 us; the launch traced here: 155 us
  Pallas kernels  154 us (99%)
    pallas_call x1, Pallas kernels, exchange(): pl.pallas_call(exchange_kernel, out_shape=(jax.ShapeDtypeStruct((TOK, FEA...  138 us
    pallas_call x1, Pallas kernels, precondition(): pl.pallas_call(precondition_kernel, grid=(2,), out_shape=(jax.ShapeDtypeS...  15.5 us

profile of v3, /device:TPU:0, one launch (start us, length us, event | category | flops | bytes accessed | tf_op | source)
XLA Modules:
  0.0 155.0 jit_solution(18040176438677499703)
XLA Ops:
  0.6 138.1 %exchange.1 = (bf16[1024,256]{1,0:T(8,128)(2,1)}, f32[2,512,512]{2,1,0:T(8,128)}) custom-call(bf16[1024,256]{1,0:T(8,128)(2,1)} %tok_ref.1, bf16[512,1024]{1,0:T(8,128)(2,1)} %w_ref.1, bf16[1024,1024]{1,0:T(8,128)(2,1)} %cot_ref.1), custom_call_target="tpu_custom_call" | custom-call | flops 25769803776 | bytes 16777216 | tf_op jit(solution)/shard_map/exchange/pallas_call | solution.py:474
  138.7 0.0 copy-start
  138.7 15.5 %precondition.1 = (bf16[512,1024]{1,0:T(8,128)(2,1)}, f32[1,2,512,512]{3,2,1,0:T(8,128)}, f32[1,2,512,512]{3,2,1,0:T(8,128)}) custom-call(f32[2,512,512]{2,1,0:T(8,128)} %get-tuple-element.10.gt_ref, f32[1,2,512,512]{3,2,1,0:T(8,128)} %left_ref.1, f32[1,2,512,512]{3,2,1,0:T(8,128)} %right_ref.1), custom_call_target="tpu_custom_call" | custom-call | tf_op jit(solution)/shard_map/precondition/pallas_call | solution.py:573
  154.2 0.0 copy-done
  154.2 0.8 copy.10
Async XLA Ops:
  138.7 15.5 %copy-start = (bf16[1024,256]{1,0:T(8,128)(2,1)S(1)}, bf16[1024,256]{1,0:T(8,128)(2,1)}, u32[]{:S(2)}) copy-start(bf16[1024,256]{1,0:T(8,128)(2,1)} %get-tuple-element.18) | copy-start | bytes 1572868

commit v4 on v3

--- a/solution.py
+++ b/solution.py
@@ -53,10 +53,14 @@
     lax.fori_loop(0, rows // chunk, body, 0)
 
 
+def total_of(values):
+    return jnp.sum(jnp.sum(values, axis=1, keepdims=True), axis=0, keepdims=True)
+
+
 def exchange_kernel(
-    tok_ref, w_ref, cot_ref, tg_ref, gt_ref,
+    tok_ref, w_ref, cot_ref, left_ref, right_ref, tg_ref, gt_ref, up_ref, lnew_ref, rnew_ref,
     wf, tok, hg, hgt, hid, part, dout,
-    s1, s1z, s2, s2z, rz, rx, sib, t1, t2, tx,
+    s1, s1z, s2, s2z, rz, rx, sib, t1, t2, tx, gt0, stat, work,
     ss, rs, ls,
 ):
     dp = lax.axis_index("dp")
@@ -347,17 +351,18 @@
 
     def g_final(h):
         q = gstate[h]
+        out = gt0 if h == 0 else gt_ref
         for k, rows, name in ((0, ZA, "a"), (1, ZB, "b")):
             got(q["z2p" + name], q["z2m" + name])
             add_rows(
-                gt_ref.at[h, pl.ds(rows[0], rows[1]), :],
+                out.at[pl.ds(rows[0], rows[1]), :],
                 (ppart(h, z, l, rows), s2z.at[h, UP, k], s2z.at[h, DN, k]),
                 rows[1],
             )
         for k, rows, name in ((0, XA, "a"), (1, XB, "b")):
             got(q["2p" + name, OWN], q["2m" + name, OWN], q["x" + name])
             add_rows(
-                gt_ref.at[h, pl.ds(rows[0], rows[1]), :],
+                out.at[pl.ds(rows[0], rows[1]), :],
                 (ppart(h, z, l, rows), s2.at[h, UP, OWN, k], s2.at[h, DN, OWN, k], rx.at[h, k]),
                 rows[1],
             )
@@ -403,30 +408,119 @@
                 TOK // 2,
             )
 
+    def newton(h):
+        early = [copy for q in (*wstate, tq) for copy in q.values()]
+        for copy in early:
+            copy.wait_send()
+        released.extend(early)
+        for copy in held:
+            copy.wait()
+
+        slots = iter(
+            [wf.at[pl.ds(i * BLK, BLK), pl.ds(j * BLK, BLK)] for i in range(8) for j in range(2)]
+            + [tok.at[pl.ds(0, BLK), pl.ds(j * BLK, BLK)] for j in range(8)]
+        )
+        gh, gth, lp = next(slots), next(slots), next(slots)
+        mh, zs, cr, fo, tw, tq2, tc, tf, root = [(next(slots), next(slots)) for _ in range(9)]
+        pieces = [pl.ds(i * 256, 256) for i in range(2)]
+        ids = lax.broadcasted_iota(jnp.int32, (256, BLK), 0)
+        across = lax.broadcasted_iota(jnp.int32, (256, BLK), 1)
+        eyes = [jnp.where(ids + i * 256 == across, 1.0, 0.0).astype(F32) for i in range(2)]
+        share = (1.0 - decay_rate) / BLK
+
+        gth[...] = gt0[...].astype(BF16)
+        gh[...] = gt0[...].T.astype(BF16)
+        trace, norm = [0.0, 0.0], [0.0, 0.0]
+        for i, rows in enumerate(pieces):
+            for side, (a, b) in enumerate(((gh, gth), (gth, gh))):
+                new = decay_rate * stat[side, rows, :] + share * dot(a[rows, :], b[...])
+                stat[side, rows, :] = new
+                trace[side] += total_of(new * eyes[i])
+                norm[side] += total_of(new * new)
+        for side, out in enumerate((lnew_ref, rnew_ref)):
+            back = pltpu.make_async_copy(stat.at[side], out, ls.at[5 + side])
+            back.start()
+            backs.append(back)
+        scale = [None, None]
+        for side in range(2):
+            ridge = ridge_share * trace[side] / BLK
+            full = norm[side] + 2.0 * ridge * trace[side] + BLK * ridge * ridge
+            scale[side] = jnp.sqrt(full) / 4.0
+            for i, rows in enumerate(pieces):
+                first = (stat[side, rows, :] + ridge * eyes[i]) / scale[side]
+                work[side, rows, :] = first
+                mh[side][rows, :] = first.astype(BF16)
+        for i, rows in enumerate(pieces):
+            for side in range(2):
+                first = work[side, rows, :]
+                square = dot(mh[side][rows, :], mh[side][...])
+                zs[side][rows, :] = (1.5625 * eyes[i] - 0.625 * first + 0.0625 * square).astype(BF16)
+                cr[side][rows, :] = (1.25 * first - 0.25 * square).astype(BF16)
+        for rows in pieces:
+            for side in range(2):
+                fo[side][rows, :] = dot(zs[side][rows, :], zs[side][...]).astype(BF16)
+        for i, rows in enumerate(pieces):
+            for side in range(2):
+                two = (
+                    1.5625 * eyes[i]
+                    - 0.3125 * work[side, rows, :]
+                    - 0.25 * dot(fo[side][rows, :], cr[side][...])
+                )
+                work[side, rows, :] = two
+                tw[side][rows, :] = two.astype(BF16)
+        for rows in pieces:
+            for side in range(2):
+                tq2[side][rows, :] = dot(tw[side][rows, :], tw[side][...]).astype(BF16)
+                tc[side][rows, :] = dot(tw[side][rows, :], mh[side][...]).astype(BF16)
+        for rows in pieces:
+            for side in range(2):
+                tf[side][rows, :] = dot(tq2[side][rows, :], tq2[side][...]).astype(BF16)
+        for rows in pieces:
+            for side in range(2):
+                three = 1.25 * work[side, rows, :] - 0.25 * dot(tf[side][rows, :], tc[side][...])
+                root[side][rows, :] = (lax.rsqrt(jnp.sqrt(scale[side])) * three).astype(BF16)
+        for rows in pieces:
+            lp[rows, :] = dot(root[0][rows, :], gh[...]).astype(BF16)
+        raw_sum, grad_sum = 0.0, 0.0
+        for rows in pieces:
+            raw = dot(lp[rows, :], root[1][...])
+            work[0, rows, :] = raw
+            raw_sum += total_of(raw * raw)
+            grad_sum += total_of(gt0[rows, :] * gt0[rows, :])
+        size = float(BLK * BLK)
+        ratio = jnp.sqrt(grad_sum / size) / jnp.sqrt(raw_sum / size + epsilon)
+        for rows in pieces:
+            up_ref[rows, :] = (work[0, rows, :] * ratio).astype(BF16)
+
     local = [
         pltpu.make_async_copy(w_ref, wf.at[rows_of(z, l, (0, BLK)), :], ls.at[0]),
         pltpu.make_async_copy(tok_ref, tok.at[:, tcols(xh, y, c)], ls.at[1]),
         pltpu.make_async_copy(cot_ref, hg, ls.at[2]),
     ]
+    held = [
+        pltpu.make_async_copy(left_ref.at[0, 0], stat.at[0], ls.at[3]),
+        pltpu.make_async_copy(right_ref.at[0, 0], stat.at[1], ls.at[4]),
+    ]
+    backs, released = [], []
     w_own(0, True)
     w_own(0, False)
     t_own()
     t_forward_own()
-    for copy in local:
+    for copy in local + held:
         copy.start()
     w_forward_own(0)
     w_own(1, True)
     w_last(0)
     w_partner(0)
     w_cross(0)
+    t_share_own()
+    t_last_own()
     t_partner()
     w_own(1, False)
     w_forward_partner(0)
     w_forward_own(1)
-    t_last_own()
     w_partner(1)
     t_forward_partner()
-    t_share_own()
     w_cross(1)
     w_done(0)
     t_last()
@@ -440,8 +534,8 @@
     gradient(0)
     g_start(0)
     w_done(1)
+    hidden(1, 1)
     hidden(1, 0)
-    hidden(1, 1)
     input_other(0)
     g_second(0)
     gradient(1)
@@ -450,8 +544,8 @@
     g_start(1)
     input_other(1)
     input_own(1)
+    d_first(1)
     g_cross(0)
-    d_first(1)
     g_second(1)
     d_second()
     g_cross(1)
@@ -461,24 +555,32 @@
     g_middle(1)
     g_final(0)
     g_middle_second(1)
+    newton(0)
     g_final(1)
     d_final()
+    for copy in backs:
+        copy.wait()
     for copy in copies:
-        copy.wait_send()
-
-
-def exchange(tokens, weight, cotangent):
+        if not any(copy is other for other in released):
+            copy.wait_send()
+
+
+def exchange(tokens, weight, cotangent, left_stats, right_stats):
     any_spec = pl.BlockSpec(memory_space=pl.ANY)
     vmem_spec = pl.BlockSpec(memory_space=pltpu.VMEM)
     dma = pltpu.SemaphoreType.DMA
+    square = jax.ShapeDtypeStruct((BLK, BLK), F32)
     return pl.pallas_call(
         exchange_kernel,
         out_shape=(
             jax.ShapeDtypeStruct((TOK, FEAT), BF16),
-            jax.ShapeDtypeStruct((2, BLK, BLK), F32),
+            square,
+            jax.ShapeDtypeStruct((BLK, BLK), BF16),
+            square,
+            square,
         ),
-        in_specs=[any_spec, any_spec, any_spec],
-        out_specs=(vmem_spec, vmem_spec),
+        in_specs=[any_spec] * 5,
+        out_specs=(vmem_spec, vmem_spec, vmem_spec, any_spec, any_spec),
         scratch_shapes=[
             pltpu.VMEM((D, COLS), BF16),
             pltpu.VMEM((TOK, D), BF16),
@@ -497,26 +599,40 @@
             pltpu.VMEM((2, 2, TOK // 2, FEAT), BF16),
             pltpu.VMEM((2, 2, 2, TOK // 2, FEAT), BF16),
             pltpu.VMEM((2, TOK // 2, FEAT), BF16),
+            pltpu.VMEM((BLK, BLK), F32),
+            pltpu.VMEM((2, BLK, BLK), F32),
+            pltpu.VMEM((2, BLK, BLK), F32),
             dma((NSEM,)),
             dma((NSEM,)),
-            dma((3,)),
+            dma((7,)),
         ],
         compiler_params=pltpu.CompilerParams(
-            collective_id=0, has_side_effects=True, vmem_limit_bytes=60 * 2**20
+            collective_id=0, has_side_effects=True, vmem_limit_bytes=62 * 2**20
         ),
         cost_estimate=pl.CostEstimate(
             flops=6 * TOK * D * COLS, bytes_accessed=2**24, transcendentals=2 * TOK * COLS
         ),
         name="exchange",
-    )(tokens, weight, cotangent)
-
-
-def total_of(values):
-    return jnp.sum(jnp.sum(values, axis=1, keepdims=True), axis=0, keepdims=True)
-
-
-def precondition_kernel(gt_ref, left_ref, right_ref, update_ref, left_out, right_out):
-    gt = gt_ref[0]
+    )(tokens, weight, cotangent, left_stats, right_stats)
+
+
+def precondition_kernel(
+    gt_ref, left_ref, right_ref, tg_ref, up_ref, lnew_ref, rnew_ref,
+    tg_out, update_ref, left_out, right_out,
+    up, lnew, rnew, sems,
+):
+    def move(i, source, target):
+        copy = pltpu.make_async_copy(source, target, sems.at[i])
+        copy.start()
+        return copy
+
+    passed = [
+        move(0, tg_ref, tg_out),
+        move(1, up_ref, update_ref.at[:, pl.ds(0, BLK)]),
+        move(2, lnew_ref, left_out.at[0, 0]),
+        move(3, rnew_ref, right_out.at[0, 0]),
+    ]
+    gt = gt_ref[...]
     grad = gt.T
     gth, gh = gt.astype(BF16), grad.astype(BF16)
     rows = lax.broadcasted_iota(jnp.int32, (BLK, BLK), 0)
@@ -525,8 +641,10 @@
     share = (1.0 - decay_rate) / BLK
     left = decay_rate * left_ref[0, 0] + share * dot(gh, gth)
     right = decay_rate * right_ref[0, 0] + share * dot(gth, gh)
-    left_out[0, 0] = left
-    right_out[0, 0] = right
+    lnew[...] = left
+    rnew[...] = right
+    passed.append(move(4, lnew, left_out.at[0, 1]))
+    passed.append(move(5, rnew, right_out.at[0, 1]))
 
     def each(function, *lists):
         return [function(*items) for items in zip(*lists)]
@@ -565,30 +683,43 @@
     size = float(BLK * BLK)
     grad_rms = jnp.sqrt(total_of(gt * gt) / size)
     raw_rms = jnp.sqrt(total_of(raw * raw) / size + epsilon)
-    update_ref[...] = (raw * (grad_rms / raw_rms)).astype(BF16)
-
-
-def precondition(gt, left_stats, right_stats):
-    stat_spec = pl.BlockSpec((1, 1, BLK, BLK), lambda h: (0, h, 0, 0))
+    up[...] = (raw * (grad_rms / raw_rms)).astype(BF16)
+    passed.append(move(6, up, update_ref.at[:, pl.ds(BLK, BLK)]))
+    for copy in passed:
+        copy.wait()
+
+
+def precondition(gt, left_stats, right_stats, tokens_grad, up, left_new, right_new):
+    any_spec = pl.BlockSpec(memory_space=pl.ANY)
+    stat_spec = pl.BlockSpec((1, 1, BLK, BLK), lambda i: (0, 1, 0, 0))
     return pl.pallas_call(
         precondition_kernel,
-        grid=(2,),
+        grid=(1,),
         out_shape=(
+            jax.ShapeDtypeStruct((TOK, FEAT), BF16),
             jax.ShapeDtypeStruct((BLK, COLS), BF16),
             jax.ShapeDtypeStruct(left_stats.shape, F32),
             jax.ShapeDtypeStruct(right_stats.shape, F32),
         ),
-        in_specs=[pl.BlockSpec((1, BLK, BLK), lambda h: (h, 0, 0)), stat_spec, stat_spec],
-        out_specs=(pl.BlockSpec((BLK, BLK), lambda h: (0, h)), stat_spec, stat_spec),
-        compiler_params=pltpu.CompilerParams(vmem_limit_bytes=56 * 2**20),
+        in_specs=[pl.BlockSpec((BLK, BLK), lambda i: (0, 0)), stat_spec, stat_spec]
+        + [any_spec] * 4,
+        out_specs=(any_spec,) * 4,
+        scratch_shapes=[
+            pltpu.VMEM((BLK, BLK), BF16),
+            pltpu.VMEM((BLK, BLK), F32),
+            pltpu.VMEM((BLK, BLK), F32),
+            pltpu.SemaphoreType.DMA((7,)),
+        ],
+        compiler_params=pltpu.CompilerParams(vmem_limit_bytes=48 * 2**20),
         name="precondition",
-    )(gt, left_stats, right_stats)
+    )(gt, left_stats, right_stats, tokens_grad, up, left_new, right_new)
 
 
 def shards(tokens, weight, cotangent, left_stats, right_stats):
-    tokens_grad, gt = exchange(tokens, weight, cotangent)
-    update, left_new, right_new = precondition(gt, left_stats, right_stats)
-    return tokens_grad, update, left_new, right_new
+    tokens_grad, gt, up, left_half, right_half = exchange(
+        tokens, weight, cotangent, left_stats, right_stats
+    )
+    return precondition(gt, left_stats, right_stats, tokens_grad, up, left_half, right_half)
 
 
 def solution(mesh):

time: 156 us -> 155 us (level)
  Pallas kernels: 154 us -> 147 us
  local copies, waits for them, and re-layouts: 0.8 us -> 5.75 us
    pallas_call x1, Pallas kernels: 15.5 us -> 9.17 us  [precondition(): pl.pallas_call(precondition_kernel, grid=(1,), out_shape=(jax.ShapeDtypeS...]
    unnamed x3 -> x10, local copies, waits for them, and re-layouts: 0.8 us -> 5.75 us
where the time goes in v4:
time: 155 us; the launch traced here: 153 us
  Pallas kernels  147 us (95%)
  local copies, waits for them, and re-layouts  5.75 us (4%)
    pallas_call x1, Pallas kernels, exchange(): pl.pallas_call(exchange_kernel, out_shape=(jax.ShapeDtypeStruct((TOK, FEA...  138 us
    pallas_call x1, Pallas kernels, precondition(): pl.pallas_call(precondition_kernel, grid=(1,), out_shape=(jax.ShapeDtypeS...  9.17 us
    unnamed x10, local copies, waits for them, and re-layouts  5.75 us

profile of v4, /device:TPU:0, one launch (start us, length us, event | category | flops | bytes accessed | tf_op | source)
XLA Modules:
  0.0 153.5 jit_solution(14236574631406531475)
XLA Ops:
  0.6 137.8 %exchange.1 = (bf16[1024,256]{1,0:T(8,128)(2,1)}, f32[512,512]{1,0:T(8,128)}, bf16[512,512]{1,0:T(8,128)(2,1)}, f32[512,512]{1,0:T(8,128)}, f32[512,512]{1,0:T(8,128)}) custom-call(bf16[1024,256]{1,0:T(8,128)(2,1)} %tok_ref.1, bf16[512,1024]{1,0:T(8,128)(2,1)} %w_ref.1, bf16[1024,1024]{1,0:T(8,128)(2,1)} %cot_ref.1, f32[1,2,512,512]{3,2,1,0:T(8,128)} %left_ref.3, ...), custom_call_target="tpu_custom_call" | custom-call | flops 25769803776 | bytes 16777216 | tf_op jit(solution)/shard_map/exchange/pallas_call | solution.py:573
  138.4 0.0 copy-start
  138.4 1.2 copy-done
  139.6 0.0 copy-start.1
  139.6 1.2 copy-done.1
  140.9 0.0 copy-start.2
  140.9 1.2 copy-done.2
  142.1 0.0 copy-start.3
  142.1 1.0 copy-done.3
  143.1 0.0 copy-start.4
  143.1 1.0 copy-done.4
  144.2 9.2 %precondition.1 = (bf16[1024,256]{1,0:T(8,128)(2,1)}, bf16[512,1024]{1,0:T(8,128)(2,1)}, f32[1,2,512,512]{3,2,1,0:T(8,128)}, f32[1,2,512,512]{3,2,1,0:T(8,128)}) custom-call(f32[512,512]{1,0:T(8,128)S(1)} %copy-done, f32[1,2,512,512]{3,2,1,0:T(8,128)} %left_ref.3, f32[1,2,512,512]{3,2,1,0:T(8,128)} %right_ref.3, bf16[1024,256]{1,0:T(8,128)(2,1)S(1)} %copy-done.3, ...), custom_call_target="tpu_custom_call" | custom-call | tf_op jit(solution)/shard_map/precondition/pallas_call | solution.py:695
Async XLA Ops:
  138.4 1.2 copy-start
  139.6 1.2 copy-start.1
  140.9 1.2 copy-start.2
  142.1 1.0 copy-start.3
  143.1 1.0 copy-start.4

commit v5 on v4

--- a/solution.py
+++ b/solution.py
@@ -27,7 +27,8 @@
 ZZ = (176, 160)
 HA = (0, 256)
 HB = (256, 256)
-NSEM = 160
+N_SEND = 86
+N_RECV = 126
 
 
 def dot(a, b):
@@ -83,17 +84,25 @@
         pl.semaphore_signal(barrier, inc=1, device_id=dev, device_id_type=MESH)
     pl.semaphore_wait(barrier, 7)
 
-    copies = []
+    copies, pending = [], []
+    unused = list(range(N_SEND))
 
     def send(src, dst, dev):
-        k = len(copies)
+        k = unused.pop(0)
         copy = pltpu.make_async_remote_copy(
-            src_ref=src, dst_ref=dst, send_sem=ss.at[k], recv_sem=rs.at[k],
+            src_ref=src, dst_ref=dst, send_sem=ss.at[k], recv_sem=rs.at[len(copies)],
             device_id=dev, device_id_type=MESH,
         )
         copy.start()
         copies.append(copy)
+        pending.append((copy, k))
         return copy
+
+    def release():
+        for copy, k in pending:
+            copy.wait_send()
+            unused.append(k)
+        pending.clear()
 
     def got(*several):
         for copy in several:
@@ -244,7 +253,7 @@
                 hg[big, cols] = (cot * gelu_slope(hid[small, :])).astype(BF16)
                 return inner
 
-            lax.fori_loop(0, 16, slope, 0)
+            lax.fori_loop(0, 16, slope, 0, unroll=4)
             return carry
 
         lax.fori_loop(2 * r, 2 * r + 2, tile, 0)
@@ -260,7 +269,7 @@
             part[h, d] = (dot(hgt[...], tok[:, at]) * grad_scale).astype(BF16)
             return carry
 
-        lax.fori_loop(0, 8, block, 0)
+        lax.fori_loop(0, 8, block, 0, unroll=8)
 
     def wide_dot(rows, g):
         at = pl.ds(pl.multiple_of(g * FEAT, FEAT), FEAT)
@@ -275,7 +284,7 @@
             dout[t, rows, :] = wide_dot(rows, t * 2 + oc).astype(BF16)
             return carry
 
-        lax.fori_loop(0, 8, block, 0)
+        lax.fori_loop(0, 8, block, 0, unroll=8)
         dq["c", r] = send(dout.at[:, rows, :], sib.at[:, rows, :], dev_c)
 
     def input_own(r):
@@ -287,7 +296,7 @@
             sib[t, rows, :] = mine.astype(BF16)
             return carry
 
-        lax.fori_loop(0, 8, block, 0)
+        lax.fori_loop(0, 8, block, 0, unroll=8)
 
     def ppart(h, zi, li, rows):
         return part.at[h, zi * 2 + li, pl.ds(rows[0], rows[1]), :]
@@ -409,10 +418,6 @@
             )
 
     def newton(h):
-        early = [copy for q in (*wstate, tq) for copy in q.values()]
-        for copy in early:
-            copy.wait_send()
-        released.extend(early)
         for copy in held:
             copy.wait()
 
@@ -501,68 +506,67 @@
         pltpu.make_async_copy(left_ref.at[0, 0], stat.at[0], ls.at[3]),
         pltpu.make_async_copy(right_ref.at[0, 0], stat.at[1], ls.at[4]),
     ]
-    backs, released = [], []
+    backs = []
+    w_own(1, False)
+    t_own()
     w_own(0, True)
-    w_own(0, False)
-    t_own()
     t_forward_own()
     for copy in local + held:
         copy.start()
+    w_own(1, True)
     w_forward_own(0)
-    w_own(1, True)
+    w_own(0, False)
+    t_last_own()
+    w_partner(0)
     w_last(0)
-    w_partner(0)
+    w_forward_own(1)
+    t_partner()
     w_cross(0)
-    t_share_own()
-    t_last_own()
-    t_partner()
-    w_own(1, False)
     w_forward_partner(0)
-    w_forward_own(1)
     w_partner(1)
     t_forward_partner()
+    t_last()
+    t_share_own()
+    w_last(1)
+    t_done()
+    w_done(0)
     w_cross(1)
-    w_done(0)
-    t_last()
-    t_done()
     for copy in local:
         copy.wait()
-    hidden(0, 1)
     hidden(0, 0)
     w_forward_partner(1)
-    w_last(1)
+    hidden(0, 1)
     gradient(0)
     g_start(0)
     w_done(1)
-    hidden(1, 1)
     hidden(1, 0)
     input_other(0)
-    g_second(0)
-    gradient(1)
+    hidden(1, 1)
+    input_other(1)
     input_own(0)
     d_first(0)
+    g_second(0)
+    release()
+    gradient(1)
+    g_middle(0)
     g_start(1)
-    input_other(1)
     input_own(1)
     d_first(1)
     g_cross(0)
+    d_second()
+    g_middle_second(0)
     g_second(1)
-    d_second()
+    d_cross()
+    g_final(0)
+    g_middle(1)
     g_cross(1)
-    g_middle(0)
-    g_middle_second(0)
-    d_cross()
-    g_middle(1)
-    g_final(0)
+    newton(0)
     g_middle_second(1)
-    newton(0)
+    d_final()
     g_final(1)
-    d_final()
     for copy in backs:
         copy.wait()
-    for copy in copies:
-        if not any(copy is other for other in released):
-            copy.wait_send()
+    release()
 
 
 def exchange(tokens, weight, cotangent, left_stats, right_stats):
@@ -602,8 +606,8 @@
             pltpu.VMEM((BLK, BLK), F32),
             pltpu.VMEM((2, BLK, BLK), F32),
             pltpu.VMEM((2, BLK, BLK), F32),
-            dma((NSEM,)),
-            dma((NSEM,)),
+            dma((N_SEND,)),
+            dma((N_RECV,)),
             dma((7,)),
         ],
         compiler_params=pltpu.CompilerParams(
@@ -619,19 +623,21 @@
 def precondition_kernel(
     gt_ref, left_ref, right_ref, tg_ref, up_ref, lnew_ref, rnew_ref,
     tg_out, update_ref, left_out, right_out,
-    up, lnew, rnew, sems,
+    up, lnew, rnew, tg_held, up_held, l_held, r_held, sems,
 ):
     def move(i, source, target):
         copy = pltpu.make_async_copy(source, target, sems.at[i])
         copy.start()
         return copy
 
-    passed = [
-        move(0, tg_ref, tg_out),
-        move(1, up_ref, update_ref.at[:, pl.ds(0, BLK)]),
-        move(2, lnew_ref, left_out.at[0, 0]),
-        move(3, rnew_ref, right_out.at[0, 0]),
-    ]
+    holds = (
+        (tg_ref, tg_held, tg_out),
+        (up_ref, up_held, update_ref.at[:, pl.ds(0, BLK)]),
+        (lnew_ref, l_held, left_out.at[0, 0]),
+        (rnew_ref, r_held, right_out.at[0, 0]),
+    )
+    arriving = [move(i, source, held) for i, (source, held, _) in enumerate(holds)]
+    passed = []
     gt = gt_ref[...]
     grad = gt.T
     gth, gh = gt.astype(BF16), grad.astype(BF16)
@@ -643,6 +649,9 @@
     right = decay_rate * right_ref[0, 0] + share * dot(gth, gh)
     lnew[...] = left
     rnew[...] = right
+    for i, (copy, (_, held, target)) in enumerate(zip(arriving, holds)):
+        copy.wait()
+        passed.append(move(7 + i, held, target))
     passed.append(move(4, lnew, left_out.at[0, 1]))
     passed.append(move(5, rnew, right_out.at[0, 1]))
 
@@ -708,9 +717,13 @@
             pltpu.VMEM((BLK, BLK), BF16),
             pltpu.VMEM((BLK, BLK), F32),
             pltpu.VMEM((BLK, BLK), F32),
-            pltpu.SemaphoreType.DMA((7,)),
+            pltpu.VMEM((TOK, FEAT), BF16),
+            pltpu.VMEM((BLK, BLK), BF16),
+            pltpu.VMEM((BLK, BLK), F32),
+            pltpu.VMEM((BLK, BLK), F32),
+            pltpu.SemaphoreType.DMA((11,)),
         ],
-        compiler_params=pltpu.CompilerParams(vmem_limit_bytes=48 * 2**20),
+        compiler_params=pltpu.CompilerParams(vmem_limit_bytes=62 * 2**20),
         name="precondition",
     )(gt, left_stats, right_stats, tokens_grad, up, left_new, right_new)
 

time: 155 us -> 150 us (0.968); the launches traced: 153 us -> 150 us
  local copies, waits for them, and re-layouts: 5.75 us -> 0 us
  Pallas kernels: 147 us -> 149 us
    unnamed x10 -> x0, local copies, waits for them, and re-layouts: 5.75 us -> none
where the time goes in v5:
time: 150 us
  Pallas kernels  149 us (99%)
    pallas_call x1, Pallas kernels, exchange(): pl.pallas_call(exchange_kernel, out_shape=(jax.ShapeDtypeStruct((TOK, FEA...  139 us
    pallas_call x1, Pallas kernels, precondition(): pl.pallas_call(precondition_kernel, grid=(1,), out_shape=(jax.ShapeDtypeS...  10.3 us

profile of v5, /device:TPU:0, one launch (start us, length us, event | category | flops | bytes accessed | tf_op | source)
XLA Modules:
  0.0 150.3 jit_solution(15653659759166036018)
XLA Ops:
  0.6 139.1 %exchange.1 = (bf16[1024,256]{1,0:T(8,128)(2,1)}, f32[512,512]{1,0:T(8,128)}, bf16[512,512]{1,0:T(8,128)(2,1)}, f32[512,512]{1,0:T(8,128)}, f32[512,512]{1,0:T(8,128)}) custom-call(bf16[1024,256]{1,0:T(8,128)(2,1)} %tok_ref.1, bf16[512,1024]{1,0:T(8,128)(2,1)} %w_ref.1, bf16[1024,1024]{1,0:T(8,128)(2,1)} %cot_ref.1, f32[1,2,512,512]{3,2,1,0:T(8,128)} %left_ref.3, ...), custom_call_target="tpu_custom_call" | custom-call | flops 25769803776 | bytes 16777216 | tf_op jit(solution)/shard_map/exchange/pallas_call | solution.py:577
  139.8 10.3 %precondition.1 = (bf16[1024,256]{1,0:T(8,128)(2,1)}, bf16[512,1024]{1,0:T(8,128)(2,1)}, f32[1,2,512,512]{3,2,1,0:T(8,128)}, f32[1,2,512,512]{3,2,1,0:T(8,128)}) custom-call(f32[512,512]{1,0:T(8,128)} %get-tuple-element.9.gt_ref, f32[1,2,512,512]{3,2,1,0:T(8,128)} %left_ref.3, f32[1,2,512,512]{3,2,1,0:T(8,128)} %right_ref.3, ...), custom_call_target="tpu_custom_call" | custom-call | tf_op jit(solution)/shard_map/precondition/pallas_call | solution.py:704

commit v6 on v5

--- a/solution.py
+++ b/solution.py
@@ -636,6 +636,10 @@
         (lnew_ref, l_held, left_out.at[0, 0]),
         (rnew_ref, r_held, right_out.at[0, 0]),
     )
+    olds = [
+        move(11, left_ref.at[0, 1], lnew),
+        move(12, right_ref.at[0, 1], rnew),
+    ]
     arriving = [move(i, source, held) for i, (source, held, _) in enumerate(holds)]
     passed = []
     gt = gt_ref[...]
@@ -645,8 +649,11 @@
     cols = lax.broadcasted_iota(jnp.int32, (BLK, BLK), 1)
     eye = jnp.where(rows == cols, 1.0, 0.0).astype(F32)
     share = (1.0 - decay_rate) / BLK
-    left = decay_rate * left_ref[0, 0] + share * dot(gh, gth)
-    right = decay_rate * right_ref[0, 0] + share * dot(gth, gh)
+    left, right = share * dot(gh, gth), share * dot(gth, gh)
+    for copy in olds:
+        copy.wait()
+    left = decay_rate * lnew[...] + left
+    right = decay_rate * rnew[...] + right
     lnew[...] = left
     rnew[...] = right
     for i, (copy, (_, held, target)) in enumerate(zip(arriving, holds)):
@@ -700,7 +707,6 @@
 
 def precondition(gt, left_stats, right_stats, tokens_grad, up, left_new, right_new):
     any_spec = pl.BlockSpec(memory_space=pl.ANY)
-    stat_spec = pl.BlockSpec((1, 1, BLK, BLK), lambda i: (0, 1, 0, 0))
     return pl.pallas_call(
         precondition_kernel,
         grid=(1,),
@@ -710,8 +716,7 @@
             jax.ShapeDtypeStruct(left_stats.shape, F32),
             jax.ShapeDtypeStruct(right_stats.shape, F32),
         ),
-        in_specs=[pl.BlockSpec((BLK, BLK), lambda i: (0, 0)), stat_spec, stat_spec]
-        + [any_spec] * 4,
+        in_specs=[pl.BlockSpec((BLK, BLK), lambda i: (0, 0))] + [any_spec] * 6,
         out_specs=(any_spec,) * 4,
         scratch_shapes=[
             pltpu.VMEM((BLK, BLK), BF16),
@@ -721,7 +726,7 @@
             pltpu.VMEM((BLK, BLK), BF16),
             pltpu.VMEM((BLK, BLK), F32),
             pltpu.VMEM((BLK, BLK), F32),
-            pltpu.SemaphoreType.DMA((11,)),
+            pltpu.SemaphoreType.DMA((13,)),
         ],
         compiler_params=pltpu.CompilerParams(vmem_limit_bytes=62 * 2**20),
         name="precondition",

time: 150 us -> 151 us (level)
  no operation moved by 1% of the time
where the time goes in v6:
time: 151 us; the launch traced here: 150 us
  Pallas kernels  150 us (99%)
    pallas_call x1, Pallas kernels, exchange(): pl.pallas_call(exchange_kernel, out_shape=(jax.ShapeDtypeStruct((TOK, FEA...  139 us
    pallas_call x1, Pallas kernels, precondition(): pl.pallas_call(precondition_kernel, grid=(1,), out_shape=(jax.ShapeDtypeS...  10.4 us

profile of v6, /device:TPU:0, one launch (start us, length us, event | category | flops | bytes accessed | tf_op | source)
XLA Modules:
  0.0 150.4 jit_solution(9713688800024117864)
XLA Ops:
  0.6 139.1 %exchange.1 = (bf16[1024,256]{1,0:T(8,128)(2,1)}, f32[512,512]{1,0:T(8,128)}, bf16[512,512]{1,0:T(8,128)(2,1)}, f32[512,512]{1,0:T(8,128)}, f32[512,512]{1,0:T(8,128)}) custom-call(bf16[1024,256]{1,0:T(8,128)(2,1)} %tok_ref.1, bf16[512,1024]{1,0:T(8,128)(2,1)} %w_ref.1, bf16[1024,1024]{1,0:T(8,128)(2,1)} %cot_ref.1, f32[1,2,512,512]{3,2,1,0:T(8,128)} %left_ref.3, ...), custom_call_target="tpu_custom_call" | custom-call | flops 25769803776 | bytes 16777216 | tf_op jit(solution)/shard_map/exchange/pallas_call | solution.py:577
  139.8 10.4 %precondition.1 = (bf16[1024,256]{1,0:T(8,128)(2,1)}, bf16[512,1024]{1,0:T(8,128)(2,1)}, f32[1,2,512,512]{3,2,1,0:T(8,128)}, f32[1,2,512,512]{3,2,1,0:T(8,128)}) custom-call(f32[512,512]{1,0:T(8,128)} %get-tuple-element.9.gt_ref, f32[1,2,512,512]{3,2,1,0:T(8,128)} %left_ref.3, f32[1,2,512,512]{3,2,1,0:T(8,128)} %right_ref.3, ...), custom_call_target="tpu_custom_call" | custom-call | tf_op jit(solution)/shard_map/precondition/pallas_call | solution.py:710

commit v7 on v6

--- a/solution.py
+++ b/solution.py
@@ -656,9 +656,6 @@
     right = decay_rate * rnew[...] + right
     lnew[...] = left
     rnew[...] = right
-    for i, (copy, (_, held, target)) in enumerate(zip(arriving, holds)):
-        copy.wait()
-        passed.append(move(7 + i, held, target))
     passed.append(move(4, lnew, left_out.at[0, 1]))
     passed.append(move(5, rnew, right_out.at[0, 1]))
 
@@ -681,6 +678,9 @@
     )
     crossed = each(lambda a, q: (1.25 * a - 0.25 * q).astype(BF16), first, square)
     fourth = each(lambda a: dot(a, a).astype(BF16), zero_sq)
+    for i, (copy, (_, held, target)) in enumerate(zip(arriving, holds)):
+        copy.wait()
+        passed.append(move(7 + i, held, target))
     two = each(
         lambda a, f, x: 1.5625 * eye - 0.3125 * a - 0.25 * dot(f, x), first, fourth, crossed
     )

time: 151 us -> 150 us (level)
  no operation moved by 1% of the time
where the time goes in v7:
time: 150 us; the launch traced here: 149 us
  Pallas kernels  149 us (99%)
    pallas_call x1, Pallas kernels, exchange(): pl.pallas_call(exchange_kernel, out_shape=(jax.ShapeDtypeStruct((TOK, FEA...  139 us
    pallas_call x1, Pallas kernels, precondition(): pl.pallas_call(precondition_kernel, grid=(1,), out_shape=(jax.ShapeDtypeS...  9.66 us

profile of v7, /device:TPU:0, one launch (start us, length us, event | category | flops | bytes accessed | tf_op | source)
XLA Modules:
  0.0 149.4 jit_solution(7129867998963230733)
XLA Ops:
  0.6 138.9 %exchange.1 = (bf16[1024,256]{1,0:T(8,128)(2,1)}, f32[512,512]{1,0:T(8,128)}, bf16[512,512]{1,0:T(8,128)(2,1)}, f32[512,512]{1,0:T(8,128)}, f32[512,512]{1,0:T(8,128)}) custom-call(bf16[1024,256]{1,0:T(8,128)(2,1)} %tok_ref.1, bf16[512,1024]{1,0:T(8,128)(2,1)} %w_ref.1, bf16[1024,1024]{1,0:T(8,128)(2,1)} %cot_ref.1, f32[1,2,512,512]{3,2,1,0:T(8,128)} %left_ref.3, ...), custom_call_target="tpu_custom_call" | custom-call | flops 25769803776 | bytes 16777216 | tf_op jit(solution)/shard_map/exchange/pallas_call | solution.py:577
  139.5 9.7 %precondition.1 = (bf16[1024,256]{1,0:T(8,128)(2,1)}, bf16[512,1024]{1,0:T(8,128)(2,1)}, f32[1,2,512,512]{3,2,1,0:T(8,128)}, f32[1,2,512,512]{3,2,1,0:T(8,128)}) custom-call(f32[512,512]{1,0:T(8,128)} %get-tuple-element.9.gt_ref, f32[1,2,512,512]{3,2,1,0:T(8,128)} %left_ref.3, f32[1,2,512,512]{3,2,1,0:T(8,128)} %right_ref.3, ...), custom_call_target="tpu_custom_call" | custom-call | tf_op jit(solution)/shard_map/precondition/pallas_call | solution.py:710
